TPU v7x, 256 devices: a whole 4x4x8 slice. The times are simulated.
256 devices in a mesh: section: 16 (over y, x_lo, core), tp: 16 (over x_hi, z).
Axes of the slice: x: 4 (x_hi: 2, x_lo: 2; x = x_hi * 2 + x_lo), y: 4, z: 8, core: 2. Of those that a mesh axis runs over, the one named last changes fastest.
Arguments:
- saved_queries: bfloat16 [16, 512, 7168], P('section', None, 'tp'), may hold values from -40 to 40
- saved_keys: bfloat16 [16, 512, 7168], P('section', None, 'tp'), may hold values from -40 to 40
- values: bfloat16 [16, 512, 7168], P('section', None, 'tp'), may hold values from -6 to 6
- attention_output_grad: bfloat16 [16, 512, 7168], P('section', None, 'tp'), may hold values from -0.59765625 to 0.59765625
- segments: int32 [512], replicated, may hold values from 0 to 5, never falling along the last dimension, each value on 1 to 256 neighbouring positions
- hidden: bfloat16 [16, 512, 3584], P('section'), may hold values from -6 to 6
- embedding: bfloat16 [512, 3584], replicated, may hold values from -6 to 6
- section_block_index: int32 [16, 1], replicated, may hold values from 0 to 1
- shared_query_weight: bfloat16 [2, 7168, 7168], P(None, 'section', 'tp'), may hold values from -0.0625 to 0.0625
- adapter_down_factor: bfloat16 [16, 7168, 128], P('section', 'tp'), may hold values from -0.0625 to 0.0625
- adapter_up_factor: bfloat16 [16, 128, 7168], P('section', None, 'tp'), may hold values from -0.5 to 0.5
- residual: bfloat16 [16, 512, 3584], P('section', 'tp'), may hold values from -0.59765625 to 0.59765625
Outputs:
- key_grad: bfloat16 [16, 512, 7168], P('section', None, 'tp')
- value_grad: bfloat16 [16, 512, 7168], P('section', None, 'tp')
- lora_down_grad: float32 [16, 7168, 128], P('section', 'tp')
- lora_up_grad: float32 [16, 128, 7168], P('section', None, 'tp')
- query_weight_grad: float32 [2, 7168, 7168], P(None, 'section', 'tp')
- passed_grad: bfloat16 [16, 512, 3584], P('section', 'tp')
- embed_grad: float32 [512, 3584], P('tp', 'section')
All inputs are finite; a program needn't handle non-finite values.
Results may differ from a plain program's by a relative error of at most 0.017.
Values may be sent and summed in bfloat16 or wider, within the bound.
A program may use at most 128 MiB of HBM per device.

v0:
```python
import jax
import jax.numpy as jnp
from jax import lax
from jax.sharding import PartitionSpec as P

MODEL_WIDTH = 3584
HD = 224


def passed_along(array, axis, by):
    count = lax.axis_size(axis)
    pairs = [(i, i + by) for i in range(count) if 0 <= i + by < count]
    return lax.ppermute(array, axis, pairs)


def attention_grads(saved_queries, saved_keys, values, attention_output_grad, segments, head_width):
    tokens = saved_queries.shape[0]
    head_count = saved_queries.shape[1] // head_width
    score_scale = head_width ** (-0.5)
    head_shape = (tokens, head_count, head_width)
    query_heads = saved_queries.reshape(head_shape)
    key_heads = saved_keys.reshape(head_shape)
    value_heads = values.reshape(head_shape)
    grad_heads = attention_output_grad.reshape(head_shape)
    scores = (
        jnp.einsum("thd,shd->hts", query_heads, key_heads, preferred_element_type=jnp.float32)
        * score_scale
    )
    positions = jnp.arange(tokens)
    allowed = (positions[:, None] >= positions[None, :]) & (segments[:, None] == segments[None, :])
    scores = jnp.where(allowed[None], scores, -1e30)
    row_top = jnp.max(scores, axis=2, keepdims=True)
    expsum = jnp.exp(scores - row_top)
    soft_weights = expsum / jnp.sum(expsum, axis=2, keepdims=True)
    probs_low = soft_weights.astype(jnp.bfloat16)
    attended = jnp.einsum(
        "hts,shd->thd", probs_low, value_heads, preferred_element_type=jnp.float32
    )
    row_delta = jnp.sum(grad_heads.astype(jnp.float32) * attended, axis=2)
    prob_grad = jnp.einsum(
        "thd,shd->hts", grad_heads, value_heads, preferred_element_type=jnp.float32
    )
    score_low = (soft_weights * (prob_grad - row_delta.T[:, :, None])).astype(jnp.bfloat16)
    query_gradient = (
        jnp.einsum("hts,shd->thd", score_low, key_heads, preferred_element_type=jnp.float32)
        * score_scale
    )
    key_grad = (
        jnp.einsum("hts,thd->shd", score_low, query_heads, preferred_element_type=jnp.float32)
        * score_scale
    )
    value_grad = jnp.einsum(
        "hts,thd->shd", probs_low, grad_heads, preferred_element_type=jnp.float32
    )
    return (
        query_gradient.reshape(tokens, -1).astype(jnp.bfloat16),
        key_grad.reshape(tokens, -1).astype(jnp.bfloat16),
        value_grad.reshape(tokens, -1).astype(jnp.bfloat16),
    )


def contract_first(left, right):
    return lax.dot_general(
        left, right, (((0,), (0,)), ((), ())), preferred_element_type=jnp.float32
    )


def contract_trailing(left, right):
    return lax.dot_general(
        left, right, (((1,), (1,)), ((), ())), preferred_element_type=jnp.float32
    )


def on_device(
    saved_queries,
    saved_keys,
    values,
    attention_output_grad,
    segments,
    hidden,
    embedding,
    section_block_index,
    shared_query_weight,
    adapter_down_factor,
    adapter_up_factor,
    residual,
):
    section_adapter_rank = lax.axis_index("section")
    tp_rank = lax.axis_index("tp")
    block_index = lax.dynamic_index_in_dim(
        section_block_index[:, 0], section_adapter_rank, keepdims=False
    )
    joined_pieces = jnp.concatenate([hidden[0], embedding], axis=1)
    column_slab_width = adapter_down_factor.shape[1]
    column_slab_start = tp_rank * column_slab_width
    local_input_rows = lax.dynamic_slice_in_dim(
        joined_pieces, column_slab_start, column_slab_width, 1
    )
    reduced_piece = jnp.dot(
        local_input_rows, adapter_down_factor[0], preferred_element_type=jnp.float32
    )
    reduced_rank_term = lax.psum(reduced_piece, "tp").astype(jnp.bfloat16)
    query_gradient, key_grad, value_grad = attention_grads(
        saved_queries[0], saved_keys[0], values[0], attention_output_grad[0], segments, HD
    )
    returned_piece = contract_trailing(query_gradient, adapter_up_factor[0])
    returned_rank = lax.psum(returned_piece, "tp").astype(jnp.bfloat16)
    up_grad = contract_first(reduced_rank_term, query_gradient)
    down_grad = contract_first(local_input_rows, returned_rank)
    adapter_columns = contract_trailing(returned_rank, adapter_down_factor[0])
    shard_piece = lax.all_gather(shared_query_weight, "section", axis=1, tiled=True)
    chosen = jnp.where(block_index == 0, shard_piece[0], shard_piece[1])
    partial_gradient = contract_trailing(query_gradient, chosen)
    owned_columns = (
        lax.dynamic_slice_in_dim(partial_gradient, column_slab_start, column_slab_width, 1)
        + adapter_columns
    )
    partial_gradient = lax.dynamic_update_slice_in_dim(
        partial_gradient, owned_columns, column_slab_start, 1
    )
    summed = lax.psum_scatter(
        partial_gradient.astype(jnp.bfloat16), "tp", scatter_dimension=0, tiled=True
    ).astype(jnp.float32)
    sent_grad = (residual[0].astype(jnp.float32) + summed[:, :MODEL_WIDTH]).astype(jnp.bfloat16)
    passed = passed_along(sent_grad, "section", -1)
    embed_part = lax.psum_scatter(
        summed[:, MODEL_WIDTH:], "section", scatter_dimension=1, tiled=True
    )
    product = contract_first(joined_pieces, query_gradient)
    gathered_grad = lax.psum_scatter(
        jnp.stack(
            [jnp.where(block_index == 0, product, 0.0), jnp.where(block_index == 1, product, 0.0)],
            axis=1,
        ).astype(jnp.bfloat16),
        "section",
        scatter_dimension=0,
        tiled=True,
    ).astype(jnp.float32)
    weight_grad = jnp.transpose(gathered_grad, (1, 0, 2))
    return (
        key_grad[None],
        value_grad[None],
        down_grad[None],
        up_grad[None],
        weight_grad,
        passed[None],
        embed_part,
    )


def solution(mesh):
    in_specs = (
        P("section", None, "tp"),
        P("section", None, "tp"),
        P("section", None, "tp"),
        P("section", None, "tp"),
        P(),
        P("section", None, None),
        P(),
        P(),
        P(None, "section", "tp"),
        P("section", "tp", None),
        P("section", None, "tp"),
        P("section", "tp", None),
    )
    out_specs = (
        P("section", None, "tp"),
        P("section", None, "tp"),
        P("section", "tp", None),
        P("section", None, "tp"),
        P(None, "section", "tp"),
        P("section", "tp", None),
        P("tp", "section"),
    )
    return jax.shard_map(
        on_device, mesh=mesh, in_specs=in_specs, out_specs=out_specs, check_vma=False
    )
```

profile of v0, /device:TPU:1, one launch (start us, length us, event | category | flops | bytes accessed | tf_op | source)
XLA Modules:
  0.0 551.3 jit_solution(580592187904876464)
XLA Ops:
  7.2 0.0 copy-start
  7.2 0.0 copy-start.10
  7.2 0.0 copy-start.8
  7.2 0.0 all-gather.2.cloned.1.call-start
  7.3 0.7 all-gather.2.cloned.1.call-update
  7.9 0.0 reduce-scatter.10.cloned.1.call-start
  8.0 1.2 fusion.37
  9.9 1.0 fusion.16
  10.9 0.0 copy-done
  10.9 3.4 fusion.36
  14.2 0.0 copy-done.10
  14.2 0.0 copy-done.8
  14.2 2.2 fusion.13
  16.4 0.0 copy-done.12
  16.5 0.5 multiply_convert_fusion
  17.0 0.4 fusion.12
  17.4 10.1 %fusion.7 = (bf16[7168,1,448]{0,2,1:T(8,128)(2,1)S(1)}, bf16[7168,1,448]{0,2,1:T(8,128)(2,1)}) fusion(pred[]{:T(512)} %bitcast.18, pred[]{:T(512)} %bitcast.20, bf16[512,448]{0,1:T(8,128)(2,1)S(1)} %bitcast.76, bf16[512,3584]{1,0:T(8,128)(2,1)} %param.18, bf16[512,3584]{1,0:T(8,128)(2,1)} %bitcast.80), kind=kOutput, calls=%fused_computation.13 | convolution fusion | flops 3309436928 | bytes 20643842 | tf_op jit(solution)/shard_map/dot_general | solution.py:63
  27.5 8.8 %pad_maximum_fusion = bf16[7168,2,448]{0,2,1:T(8,128)(2,1)} fusion(bf16[7168,1,448]{0,2,1:T(8,128)(2,1)} %get-tuple-element.24, bf16[7168,1,448]{0,2,1:T(8,128)(2,1)S(1)} %get-tuple-element.23), kind=kLoop, calls=%fused_computation.1 | loop fusion | flops 6422528 | bytes 25690112 | tf_op jit(solution)/shard_map/stack | solution.py:131
  36.2 17.6 %copy.43 = bf16[7168,896]{1,0:T(8,128)(2,1)} copy(bf16[7168,896]{0,1:T(8,128)(2,1)} %bitcast.74) | data formatting | bytes 25690112
  53.8 0.0 reduce-scatter.10.cloned.1.call-update
  53.9 0.0 reduce-scatter.8.cloned.1.call-start
  53.9 0.0 copy-start.3
  53.9 0.0 copy-start.7
  54.0 1.7 fusion.19
  55.6 0.0 copy-done.3
  55.6 0.3 fusion.25
  55.9 0.0 copy-done.7
  55.9 0.3 fusion.27
  56.3 74.6 %all-reduce.2 = (bf16[512,128]{1,0:T(8,128)(2,1)S(1)}, bf16[512,128]{1,0:T(8,128)(2,1)}) all-reduce(f32[512,128]{1,0:T(8,128)S(1)} %fusion.27, f32[512,128]{1,0:T(8,128)S(1)} %fusion.25), channel_id=1, replica_groups=mesh['section'=16,'tp'=16] {'tp'}, use_global_device_ids=true, to_apply=%region_3.4 | all-reduce | flops 131072 | bytes 786432 | tf_op jit(solution)/shard_map/psum | solution.py:107
  130.9 15.2 %fusion.3 = f32[512,7168]{1,0:T(8,128)} fusion(bf16[512,448]{0,1:T(8,128)(2,1)S(1)} %bitcast.78, bf16[2,7168,448]{2,1,0:T(8,128)(2,1)} %all-gather.2.cloned.1.call-done, pred[]{:T(512)} %bitcast.18), kind=kOutput, calls=%fused_computation.10 | convolution fusion | flops 3291545600 | bytes 27983872 | tf_op jit(solution)/shard_map/dot_general | solution.py:69
  146.1 0.0 copy-done.4
  146.1 1.7 convolution_add_fusion
  147.7 5.9 %dynamic_update_slice.3 = f32[512,7168]{1,0:T(8,128)} dynamic-update-slice(f32[512,7168]{1,0:T(8,128)} %fusion.3, f32[512,448]{1,0:T(8,128)S(1)} %convolution_add_fusion, s32[]{:T(128)} %constant.11.clone.1, s32[]{:T(128)S(6)} %select_n.39) | dynamic-update-slice | bytes 1835012 | tf_op jit(solution)/shard_map/dynamic_update_slice | solution.py:118
  153.6 9.3 %convert_element_type.92 = bf16[512,7168]{1,0:T(8,128)(2,1)} convert(f32[512,7168]{1,0:T(8,128)} %dynamic_update_slice.3) | non-fusion elementwise | flops 3670016 | bytes 22020096 | tf_op jit(solution)/shard_map/convert_element_type | solution.py:122
  162.9 0.0 reduce-scatter.8.cloned.1.call-update
  163.0 0.0 copy-start.11
  163.0 0.0 reduce-scatter.12.cloned.1.call-start
  163.0 0.0 copy-start.13
  163.0 0.8 copy-done.6
  163.8 1.0 convolution_bitcast_fusion.1
  164.8 1.0 convolution_bitcast_fusion.2
  165.8 0.0 copy-done.9
  165.8 1.3 fusion.11
  167.1 0.0 copy-done.11
  167.1 0.0 copy-done.13
  167.1 1.3 convolution_convert_fusion
  168.4 82.1 %reduce-scatter.10.cloned.1.call-done = bf16[448,896]{1,0:T(8,128)(2,1)} async-done(((bf16[7168,896]{1,0:T(8,128)(2,1)}), bf16[448,896]{1,0:T(8,128)(2,1)}) %reduce-scatter.10.cloned.1.call-update) | async-done | bytes 802832
  250.5 1.5 copy.44
  252.0 221.9 %reduce-scatter.8.cloned.1.call-done = bf16[32,7168]{1,0:T(8,128)(2,1)} async-done(((bf16[512,7168]{1,0:T(8,128)(2,1)}), bf16[32,7168]{1,0:T(8,128)(2,1)}) %reduce-scatter.8.cloned.1.call-update) | async-done | bytes 458768 | tf_op jit(solution)/shard_map/reduce_scatter | solution.py:121
  473.9 1.0 slice.19
  475.0 1.8 copy.41
  476.8 0.0 reduce-scatter.12.cloned.1.call-update
  476.8 0.0 copy-done.2
  476.8 0.1 convert_element_type.93
  476.9 0.0 copy-done.5
  476.9 0.0 copy-start.1
  476.9 0.1 fusion.20
  476.9 6.5 %collective-permute-start = (bf16[32,3584]{1,0:T(8,128)(2,1)S(1)}, bf16[32,3584]{1,0:T(8,128)(2,1)}, u32[]{:S(2)}, u32[]{:S(2)}) collective-permute-start(bf16[32,3584]{1,0:T(8,128)(2,1)S(1)} %fusion.20), channel_id=1, source_target_pairs={{16,0},{32,16},{48,32},{64,48},{80,64},{96,80},{112,96},{128,112},... | collective-permute-start | bytes 688136 | tf_op jit(solution)/shard_map/ppermute | solution.py:13
  483.4 0.2 convert_bitcast_fusion
  483.7 1.7 copy.32
  485.4 2.0 collective-permute-done
  487.4 54.2 %reduce-scatter.12.cloned.1.call-done = f32[224,32]{1,0:T(8,128)} async-done(((f32[3584,32]{1,0:T(8,128)}), f32[224,32]{1,0:T(8,128)}) %reduce-scatter.12.cloned.1.call-update) | async-done | bytes 28688
  541.6 1.6 copy.42
  543.2 1.6 copy.51
  (8 shorter events, 0.0 us)
Async XLA Ops:
  7.2 3.7 copy-start
  7.2 7.0 %copy-start.10 = (bf16[1,512,448]{1,2,0:T(8,128)(2,1)S(1)}, bf16[1,512,448]{1,2,0:T(8,128)(2,1)}, u32[]{:S(2)}) copy-start(bf16[1,512,448]{1,2,0:T(8,128)(2,1)} %param.15) | copy-start | bytes 1376260
  7.2 7.0 %copy-start.8 = (bf16[1,512,448]{1,2,0:T(8,128)(2,1)S(1)}, bf16[1,512,448]{1,2,0:T(8,128)(2,1)}, u32[]{:S(2)}) copy-start(bf16[1,512,448]{1,2,0:T(8,128)(2,1)} %param.14) | copy-start | bytes 1376260
  7.2 123.7 %all-gather.2.cloned.1.call-start = ((), (), s32[]{:S(2)}) async-start(), calls=%async_computation.3 | async-start | bytes 15597568 | tf_op jit(solution)/shard_map/all_gather | solution.py:111
  7.9 242.6 %reduce-scatter.10.cloned.1.call-start = ((), (), s32[]{:S(2)}) async-start(), calls=%async_computation.5 | async-start | bytes 13647872
  14.2 2.2 copy-start.12
  53.9 420.0 %reduce-scatter.8.cloned.1.call-start = ((), (), s32[]{:S(2)}) async-start(), calls=%async_computation.4 | async-start | bytes 7798784 | tf_op jit(solution)/shard_map/reduce_scatter | solution.py:121
  53.9 1.7 copy-start.3
  53.9 2.0 copy-start.7
  130.9 15.2 %copy-start.4 = (bf16[1,448,128]{2,1,0:T(8,128)(2,1)S(1)}, bf16[1,448,128]{2,1,0:T(8,128)(2,1)}, u32[]{:S(2)}) copy-start(bf16[1,448,128]{2,1,0:T(8,128)(2,1)} %param.21) | copy-start | bytes 344068
  162.9 0.9 copy-start.6
  162.9 2.9 copy-start.9
  163.0 4.1 copy-start.11
  163.0 378.6 %reduce-scatter.12.cloned.1.call-start = ((), (), s32[]{:S(2)}) async-start(), calls=%async_computation.6 | async-start | bytes 1949696
  163.0 4.1 copy-start.13
  168.4 308.5 %copy-start.5 = (bf16[1,32,3584]{2,1,0:T(8,128)(2,1)S(1)}, bf16[1,32,3584]{2,1,0:T(8,128)(2,1)}, u32[]{:S(2)}) copy-start(bf16[1,32,3584]{2,1,0:T(8,128)(2,1)} %param.23) | copy-start | bytes 688132
  473.9 2.9 copy-start.2
  476.9 67.9 %copy-start.1 = (bf16[1,512,448]{1,2,0:T(8,128)(2,1)S(1)}, bf16[1,512,448]{1,2,0:T(8,128)(2,1)}, u32[]{:S(2)}) copy-start(bf16[1,512,448]{1,2,0:T(8,128)(2,1)} %param.13) | copy-start | bytes 1376260
  476.9 10.4 %collective-permute-start = (bf16[32,3584]{1,0:T(8,128)(2,1)S(1)}, bf16[32,3584]{1,0:T(8,128)(2,1)}, u32[]{:S(2)}, u32[]{:S(2)}) collective-permute-start(bf16[32,3584]{1,0:T(8,128)(2,1)S(1)} %fusion.20), channel_id=1, source_target_pairs={{16,0},{32,16},{48,32},{64,48},{80,64},{96,80},{112,96},{128,112},... | collective-permute-start | bytes 688136 | tf_op jit(solution)/shard_map/ppermute | solution.py:13
Sparse Core Ops, SparseCore 0:
  9.8 93.9 all-gather.1
  106.4 144.0 reduce-scatter.9
  255.3 218.5 reduce-scatter.7
  476.9 64.6 reduce-scatter.11
where the time goes:
time: 555 us; the launch traced here: 551 us
  waiting for transfers between devices  361 us (65%)
  blocking collectives  74.6 us (13%)
  matrix products  38.5 us (7%)
  local copies, waits for them, and re-layouts  33.7 us (6%)
  other arithmetic  22.3 us (4%)
  between operations  14.6 us (3%)
  starting transfers between devices  6.64 us (1%)
    reduce_scatter x1, waiting for transfers between devices, on_device(): lax.psum_scatter(partial_gradient.astype(jnp.bfloat16), 'tp', scatter_dim...  222 us
    unnamed x6, waiting for transfers between devices  137 us
    psum x1, blocking collectives, on_device(): returned_rank = lax.psum(returned_piece, 'tp').astype(jnp.bfloat16)  74.6 us
    unnamed x34, local copies, waits for them, and re-layouts  26.7 us
    dot_general x3, matrix products, contract_trailing(): lax.dot_general(left, right, (((1,), (1,)), ((), ())), preferred_element_...  17.2 us
    dot_general x3, matrix products, contract_first(): lax.dot_general(left, right, (((0,), (0,)), ((), ())), preferred_element_...  12.1 us
  transfers between devices with their start and end apart: 5, of which 4 were waited for; matrix products, arithmetic and copies ran while one was open for 16% of the time, Pallas kernels for 0%

commit v1 on v0

v1 whole, which is shorter than its diff:
```python
import functools

import jax
import jax.numpy as jnp
from jax import lax
from jax.experimental import pallas as pl
from jax.experimental.pallas import tpu as pltpu
from jax.sharding import PartitionSpec as P

MESH = pl.DeviceIdType.MESH
TOKENS = 512
WIDTH = 3584
COLS = 448
HD = 224
RANK = 128
WIN = 512
NSEC = 16
NTP = 16
SPLIT = 128
VMEM_LIMIT = 60 * 1024 * 1024
F32 = jnp.float32
BF16 = jnp.bfloat16


def dot_nt(a, b):
    return lax.dot_general(a, b, (((1,), (1,)), ((), ())), preferred_element_type=F32)


def dot_tn(a, b):
    return lax.dot_general(a, b, (((0,), (0,)), ((), ())), preferred_element_type=F32)


def dot_nn(a, b):
    return lax.dot_general(a, b, (((1,), (0,)), ((), ())), preferred_element_type=F32)


def remote(src, dst, send_sem, recv_sem, section, tp):
    return pltpu.make_async_remote_copy(
        src_ref=src,
        dst_ref=dst,
        send_sem=send_sem,
        recv_sem=recv_sem,
        device_id={"section": section, "tp": tp},
        device_id_type=MESH,
    )


def greet(peers):
    barrier = pltpu.get_barrier_semaphore()
    for section, tp in peers:
        pl.semaphore_signal(
            barrier, inc=1, device_id={"section": section, "tp": tp}, device_id_type=MESH
        )
    pl.semaphore_wait(barrier, len(peers))


def attention(q_ref, k_ref, v_ref, g_ref, segc_ref, segr_ref, qg, kacc, vacc):
    scale = HD ** (-0.5)
    lane = lax.broadcasted_iota(jnp.int32, (1, COLS), 1)
    kacc[...] = jnp.zeros_like(kacc)
    vacc[...] = jnp.zeros_like(vacc)
    rows = 256
    for block in range(TOKENS // rows):
        top = block * rows
        cols = top + rows
        here = pl.ds(top, rows)
        upto = pl.ds(0, cols)
        row_id = lax.broadcasted_iota(jnp.int32, (rows, cols), 0) + top
        col_id = lax.broadcasted_iota(jnp.int32, (rows, cols), 1)
        allowed = (row_id >= col_id) & (segc_ref[here, :] == segr_ref[:, upto])
        dq = None
        for head in range(2):
            mask = jnp.where((lane >= HD) == (head == 1), 1.0, 0.0).astype(BF16)
            q = q_ref[here, :] * mask
            g = g_ref[here, :] * mask
            k = k_ref[upto, :]
            scores = dot_nt(q, k) * scale
            scores = jnp.where(allowed, scores, -1e30)
            top_score = jnp.max(scores, axis=1, keepdims=True)
            expo = jnp.exp(scores - top_score)
            probs = expo / jnp.sum(expo, axis=1, keepdims=True)
            low = probs.astype(BF16)
            grad = dot_nt(g, v_ref[upto, :])
            delta = jnp.sum(low.astype(F32) * grad, axis=1, keepdims=True)
            dscore = (probs * (grad - delta)).astype(BF16)
            part = dot_nn(dscore, k * mask)
            dq = part if dq is None else dq + part
            kacc[upto, :] += dot_tn(dscore, q)
            vacc[upto, :] += dot_tn(low, g)
        qg[here, :] = (dq * scale).astype(BF16)


def first_kernel(
    q_ref, k_ref, v_ref, g_ref, segc_ref, segr_ref, up_ref, hidden, weight,
    kg_ref, vg_ref, back_ref, qg4, hid4, wg,
    qg, kacc, vacc, bpart, bland, bown, ball,
    loc_sem, hs_sem, hr_sem, ws_sem, wr_sem, qs_sem, qr_sem, bs_sem, br_sem, cs_sem, cr_sem,
):
    s = lax.axis_index("section")
    t = lax.axis_index("tp")
    y, j = s // 4, s % 4
    lo, c = j // 2, j % 2
    hi, z = t // 8, t % 8
    sib = y * 4 + 2 * lo + (1 - c)
    across = [y * 4 + 2 * (1 - lo) + i for i in range(2)]
    t_far = (1 - hi) * 8 + z
    left = ((y + 3) % 4) * 4 + j
    right = ((y + 1) % 4) * 4 + j
    tp_peers = [(t + i) % NTP for i in range(1, NTP)]
    greet(
        [(sib, t), (left, t), (right, t)]
        + [(a, t) for a in across]
        + [(a, t_far) for a in across]
        + [(s, p) for p in tp_peers]
    )

    def row_block(b, owner_y):
        return wg.at[b, pl.ds(pl.multiple_of(owner_y * COLS, 64), COLS), :]

    wsends = []
    for n, (b, dest, slot) in enumerate([(0, right, 0), (1, left, 3), (1, right, 1), (0, left, 2)]):
        copy = remote(weight.at[b], row_block(b, y), ws_sem.at[n], wr_sem.at[slot], dest, t)
        copy.start()
        wsends.append(copy)

    def window(lo_d, c_d, part):
        start = pl.multiple_of(896 * lo_d + 384 * c_d + 1792 * part, 128)
        return pl.ds(start, WIN)

    hsends = []
    for part in range(2):
        for i in range(2):
            near = remote(
                hidden.at[pl.ds(0, SPLIT), window(1 - lo, i, part)],
                hid4.at[j, part, pl.ds(0, SPLIT), :],
                hs_sem.at[len(hsends)], hr_sem.at[2 + 2 * c + part], across[i], t,
            )
            near.start()
            hsends.append(near)
            far = remote(
                hidden.at[pl.ds(SPLIT, TOKENS - SPLIT), window(1 - lo, i, part)],
                hid4.at[j, part, pl.ds(SPLIT, TOKENS - SPLIT), :],
                hs_sem.at[len(hsends)], hr_sem.at[6 + 2 * c + part], across[i], t_far,
            )
            far.start()
            hsends.append(far)
        twin = remote(
            hidden.at[:, window(lo, 1 - c, part)], hid4.at[j, part],
            hs_sem.at[len(hsends)], hr_sem.at[part], sib, t,
        )
        twin.start()
        hsends.append(twin)
    locals_ = []
    for part in range(2):
        copy = pltpu.make_async_copy(
            hidden.at[:, window(lo, c, part)], hid4.at[j, part], loc_sem.at[part]
        )
        copy.start()
        locals_.append(copy)
    for b in range(2):
        copy = pltpu.make_async_copy(weight.at[b], row_block(b, y), loc_sem.at[2 + b])
        copy.start()
        locals_.append(copy)

    attention(q_ref, k_ref, v_ref, g_ref, segc_ref, segr_ref, qg, kacc, vacc)

    qsends = []
    for n, dest in enumerate([across[0], across[1], sib]):
        copy = remote(qg, qg4.at[j], qs_sem.at[n], qr_sem.at[j], dest, t)
        copy.start()
        qsends.append(copy)
    copy = pltpu.make_async_copy(qg, qg4.at[j], loc_sem.at[4])
    copy.start()
    locals_.append(copy)

    yl, yr = (y + 3) % 4, (y + 1) % 4
    yo = (y + 2) % 4

    def wait_w(b, owner_y, slot):
        remote(weight.at[b], row_block(b, owner_y), ws_sem.at[0], wr_sem.at[slot], left, t).wait_recv()

    wait_w(0, yl, 0)
    copy = remote(row_block(0, yl), row_block(0, yl), ws_sem.at[4], wr_sem.at[4], right, t)
    copy.start()
    wsends.append(copy)
    wait_w(1, yr, 3)
    copy = remote(row_block(1, yr), row_block(1, yr), ws_sem.at[5], wr_sem.at[5], left, t)
    copy.start()
    wsends.append(copy)

    bpart[...] = dot_nt(qg[...], up_ref[...]).reshape(NTP, 32, RANK)
    bsends = []
    for n, peer in enumerate(tp_peers):
        copy = remote(bpart.at[peer], bland.at[t], bs_sem.at[n], br_sem.at[t], s, peer)
        copy.start()
        bsends.append(copy)
    kg_ref[...] = (kacc[...] * HD ** (-0.5)).astype(BF16)
    vg_ref[...] = vacc[...].astype(BF16)
    bland[t] = bpart[t]
    for peer in tp_peers:
        remote(bpart.at[peer], bland.at[peer], bs_sem.at[0], br_sem.at[peer], s, peer).wait_recv()
    bown[...] = jnp.sum(bland[...], axis=0).astype(BF16)
    csends = []
    for n, peer in enumerate(tp_peers):
        copy = remote(bown, ball.at[t], cs_sem.at[n], cr_sem.at[t], s, peer)
        copy.start()
        csends.append(copy)
    ball[t] = bown[...]
    for peer in tp_peers:
        remote(bown, ball.at[peer], cs_sem.at[0], cr_sem.at[peer], s, peer).wait_recv()
    back_ref[...] = ball[...]

    for slot in [sib % 4, across[0] % 4, across[1] % 4]:
        remote(qg, qg4.at[slot], qs_sem.at[0], qr_sem.at[slot], sib, t).wait_recv()
    wait_w(1, yl, 1)
    wait_w(0, yr, 2)
    wait_w(0, yo, 4)
    wait_w(1, yo, 5)
    for part in range(2):
        remote(
            hidden.at[:, window(lo, c, part)], hid4.at[j + 1 - 2 * c, part],
            hs_sem.at[0], hr_sem.at[part], sib, t,
        ).wait_recv()
        for i in range(2):
            slot = 2 * (1 - lo) + i
            for first, count, base in ((0, SPLIT, 2), (SPLIT, TOKENS - SPLIT, 6)):
                remote(
                    hidden.at[pl.ds(first, count), window(lo, c, part)],
                    hid4.at[slot, part, pl.ds(first, count), :],
                    hs_sem.at[0], hr_sem.at[base + 2 * i + part], sib, t,
                ).wait_recv()
    for copy in locals_:
        copy.wait()
    for copy in wsends + hsends + qsends + bsends + csends:
        copy.wait_send()


def first_call(q, k, v, g, segc, segr, up, hidden, weight):
    vm = pl.BlockSpec(memory_space=pltpu.VMEM)
    anys = pl.BlockSpec(memory_space=pl.ANY)
    dma = pltpu.SemaphoreType.DMA
    return pl.pallas_call(
        first_kernel,
        out_shape=(
            jax.ShapeDtypeStruct((TOKENS, COLS), BF16),
            jax.ShapeDtypeStruct((TOKENS, COLS), BF16),
            jax.ShapeDtypeStruct((NTP, 32, RANK), BF16),
            jax.ShapeDtypeStruct((4, TOKENS, COLS), BF16),
            jax.ShapeDtypeStruct((4, 2, TOKENS, WIN), BF16),
            jax.ShapeDtypeStruct((2, 4 * COLS, COLS), BF16),
        ),
        in_specs=[vm] * 7 + [anys] * 2,
        out_specs=(vm, vm, vm, anys, anys, anys),
        scratch_shapes=[
            pltpu.VMEM((TOKENS, COLS), BF16),
            pltpu.VMEM((TOKENS, COLS), F32),
            pltpu.VMEM((TOKENS, COLS), F32),
            pltpu.VMEM((NTP, 32, RANK), F32),
            pltpu.VMEM((NTP, 32, RANK), F32),
            pltpu.VMEM((32, RANK), BF16),
            pltpu.VMEM((NTP, 32, RANK), BF16),
            dma((5,)), dma((10,)), dma((10,)), dma((6,)), dma((6,)), dma((3,)), dma((4,)),
            dma((15,)), dma((16,)), dma((15,)), dma((16,)),
        ],
        compiler_params=pltpu.CompilerParams(
            collective_id=0, has_side_effects=True, vmem_limit_bytes=VMEM_LIMIT
        ),
        name="attention_and_exchange",
    )(q, k, v, g, segc, segr, up, hidden, weight)


def input_grad_kernel(ids, qg4_ref, wh_ref, we_ref, out_ref, qsum):
    i = pl.program_id(0)

    @pl.when(i == 0)
    def _():
        qsum[...] = jnp.zeros_like(qsum)

    @pl.when(i < 4)
    def _():
        out = dot_nt(qg4_ref[0], wh_ref[0])
        out_ref[...] = out.reshape(NTP, 1, 32, 2 * COLS).astype(BF16)
        qsum[ids[i]] += qg4_ref[0].astype(F32)

    @pl.when(i == 4)
    def _():
        out = dot_nt(qsum[0].astype(BF16), we_ref[0]) + dot_nt(qsum[1].astype(BF16), we_ref[1])
        out_ref[...] = out.reshape(NTP, 1, 32, 2 * COLS).astype(BF16)


def input_grad_call(ids, qg4, wg):
    return pl.pallas_call(
        input_grad_kernel,
        grid_spec=pltpu.PrefetchScalarGridSpec(
            num_scalar_prefetch=1,
            grid=(5,),
            in_specs=[
                pl.BlockSpec((1, TOKENS, COLS), lambda i, ids: (jnp.minimum(i, 3), 0, 0)),
                pl.BlockSpec((1, 2 * COLS, COLS), lambda i, ids: (ids[jnp.minimum(i, 3)], 0, 0)),
                pl.BlockSpec((2, 2 * COLS, COLS), lambda i, ids: (0, 1, 0)),
            ],
            out_specs=pl.BlockSpec((NTP, 1, 32, 2 * COLS), lambda i, ids: (0, i, 0, 0)),
            scratch_shapes=[pltpu.VMEM((2, TOKENS, COLS), F32)],
        ),
        out_shape=jax.ShapeDtypeStruct((NTP, 5, 32, 2 * COLS), BF16),
        compiler_params=pltpu.CompilerParams(vmem_limit_bytes=VMEM_LIMIT),
        cost_estimate=pl.CostEstimate(
            flops=2 * 6 * TOKENS * COLS * 2 * COLS, bytes_accessed=12 * 2**20, transcendentals=0
        ),
        name="input_grad",
    )(ids, qg4, wg, wg)


def weight_grad_kernel(ids, qg4_ref, hid_ref, emb_ref, out_ref, acc, qsum):
    i = pl.program_id(0)
    first = pl.multiple_of(64 * ids[4], 64)

    @pl.when(i == 0)
    def _():
        qsum[...] = jnp.zeros_like(qsum)
        for n in range(4):
            qsum[ids[n]] += qg4_ref[n].astype(F32)

    @pl.when(i < 2)
    def _():
        acc[...] = jnp.zeros_like(acc)
        for n in range(4):
            acc[ids[n]] += dot_tn(hid_ref[n, 0], qg4_ref[n])

    @pl.when(i >= 2)
    def _():
        for b in range(2):
            acc[b] = dot_tn(emb_ref[0], qsum[b].astype(BF16))

    for b in range(2):
        out_ref[0, b] = acc[b, pl.ds(first, COLS), :].astype(BF16)


def weight_grad_call(ids, qg4, hid4, emb):
    return pl.pallas_call(
        weight_grad_kernel,
        grid_spec=pltpu.PrefetchScalarGridSpec(
            num_scalar_prefetch=1,
            grid=(4,),
            in_specs=[
                pl.BlockSpec((4, TOKENS, COLS), lambda i, ids: (0, 0, 0)),
                pl.BlockSpec((4, 1, TOKENS, WIN), lambda i, ids: (0, jnp.minimum(i, 1), 0, 0)),
                pl.BlockSpec((1, TOKENS, WIN), lambda i, ids: (jnp.maximum(i - 2, 0), 0, 0)),
            ],
            out_specs=pl.BlockSpec((1, 2, COLS, COLS), lambda i, ids: (i, 0, 0, 0)),
            scratch_shapes=[pltpu.VMEM((2, WIN, COLS), F32), pltpu.VMEM((2, TOKENS, COLS), F32)],
        ),
        out_shape=jax.ShapeDtypeStruct((4, 2, COLS, COLS), BF16),
        compiler_params=pltpu.CompilerParams(vmem_limit_bytes=VMEM_LIMIT),
        cost_estimate=pl.CostEstimate(
            flops=2 * 12 * TOKENS * WIN * COLS, bytes_accessed=12 * 2**20, transcendentals=0
        ),
        name="weight_grad",
    )(ids, qg4, hid4, emb)


def second_kernel(
    dw, ae, base, wsum_ref, aesum_ref, next_base,
    dwl, ael, loc_sem, ws_sem, wr_sem, as_sem, ar_sem, b_sem,
):
    s = lax.axis_index("section")
    t = lax.axis_index("tp")
    y, j = s // 4, s % 4
    peers = [(s + i) % NSEC for i in range(1, NSEC)]
    greet([(p, t) for p in peers])
    sends = []
    for n, i in enumerate((1, 3, 2)):
        yd = (y + i) % 4
        copy = remote(dw.at[yd], dwl.at[y], ws_sem.at[n], wr_sem.at[y], yd * 4 + j, t)
        copy.start()
        sends.append(copy)
    own = pltpu.make_async_copy(dw.at[y], dwl.at[y], loc_sem)
    own.start()
    copy = remote(base, next_base, b_sem.at[0], b_sem.at[1], (s + NSEC - 1) % NSEC, t)
    copy.start()
    sends.append(copy)
    for n, p in enumerate(peers):
        send = remote(ae.at[p], ael.at[s], as_sem.at[n], ar_sem.at[s], p, t)
        send.start()
        sends.append(send)
    ael[s] = ae[s]
    for p in peers:
        remote(ae.at[p], ael.at[p], as_sem.at[0], ar_sem.at[p], p, t).wait_recv()
    aesum_ref[...] = jnp.sum(ael[...], axis=0)
    copy.wait_recv()
    own.wait()
    for i in (1, 3, 2):
        ys = (y + i) % 4
        remote(dw.at[ys], dwl.at[ys], ws_sem.at[0], wr_sem.at[ys], s, t).wait_recv()
    for b in range(2):
        total = dwl[0, b].astype(F32)
        for n in range(1, 4):
            total = total + dwl[n, b].astype(F32)
        wsum_ref[b] = total
    for send in sends:
        send.wait_send()


def second_call(dw, ae, base):
    vm = pl.BlockSpec(memory_space=pltpu.VMEM)
    anys = pl.BlockSpec(memory_space=pl.ANY)
    dma = pltpu.SemaphoreType.DMA
    return pl.pallas_call(
        second_kernel,
        out_shape=(
            jax.ShapeDtypeStruct((2, COLS, COLS), F32),
            jax.ShapeDtypeStruct((32, HD), F32),
            jax.ShapeDtypeStruct((32, WIDTH), F32),
        ),
        in_specs=[anys, vm, anys],
        out_specs=(vm, vm, anys),
        scratch_shapes=[
            pltpu.VMEM((4, 2, COLS, COLS), BF16),
            pltpu.VMEM((NSEC, 32, HD), F32),
            dma, dma((3,)), dma((4,)), dma((15,)), dma((16,)), dma((2,)),
        ],
        compiler_params=pltpu.CompilerParams(
            collective_id=1, has_side_effects=True, vmem_limit_bytes=VMEM_LIMIT
        ),
        cost_estimate=pl.CostEstimate(flops=10**9, bytes_accessed=100 * 2**20, transcendentals=0),
        name="weight_sum",
    )(dw, ae, base)


def third_kernel(red, emb, pland, eland, ps_sem, pr_sem, es_sem, er_sem, loc_sem):
    s = lax.axis_index("section")
    t = lax.axis_index("tp")
    y, j = s // 4, s % 4
    peers = [(s + i) % NSEC for i in range(1, NSEC)]
    greet([(p, t) for p in peers])

    def move(src, dst, send_sem, recv_sem, here_sem, dest):
        away = remote(src, dst, send_sem, recv_sem, dest, t)
        here = pltpu.make_async_copy(src, dst, here_sem)

        @pl.when(dest != s)
        def _():
            away.start()

        @pl.when(dest == s)
        def _():
            here.start()

        def finish():
            @pl.when(dest != s)
            def _():
                away.wait_send()

            @pl.when(dest == s)
            def _():
                here.wait()

        return finish

    ends = []
    for n in range(4):
        dest = (y * 4 + n + NSEC - 1) % NSEC
        ends.append(move(red.at[n], pland.at[j], ps_sem.at[n], pr_sem.at[j], loc_sem.at[n], dest))
    for n in range(4):
        dest = 2 * j + n % 2 + 8 * (n // 2)
        ends.append(move(emb.at[n], eland.at[y], es_sem.at[n], er_sem.at[y], loc_sem.at[4 + n], dest))
    for n in range(4):
        source = (((s + 1) % NSEC) // 4) * 4 + n

        @pl.when(source != s)
        def _():
            remote(red.at[n], pland.at[n], ps_sem.at[n], pr_sem.at[n], source, t).wait_recv()

    for n in range(4):
        source = n * 4 + (s % 8) // 2

        @pl.when(source != s)
        def _():
            remote(emb.at[n], eland.at[n], es_sem.at[n], er_sem.at[n], source, t).wait_recv()

    for end in ends:
        end()


def third_call(red, emb):
    anys = pl.BlockSpec(memory_space=pl.ANY)
    dma = pltpu.SemaphoreType.DMA
    return pl.pallas_call(
        third_kernel,
        out_shape=(
            jax.ShapeDtypeStruct((4, 32, 2 * COLS), BF16),
            jax.ShapeDtypeStruct((4, 32, HD), BF16),
        ),
        in_specs=[anys, anys],
        out_specs=(anys, anys),
        scratch_shapes=[dma((4,)), dma((4,)), dma((4,)), dma((4,)), dma((8,))],
        compiler_params=pltpu.CompilerParams(
            collective_id=2, has_side_effects=True, vmem_limit_bytes=VMEM_LIMIT
        ),
        name="final_exchange",
    )(red, emb)


def on_device(
    saved_queries,
    saved_keys,
    values,
    attention_output_grad,
    segments,
    hidden,
    embedding,
    section_block_index,
    shared_query_weight,
    adapter_down_factor,
    adapter_up_factor,
    residual,
):
    s = lax.axis_index("section")
    t = lax.axis_index("tp")
    y, j = s // 4, s % 4
    lo, c = j // 2, j % 2
    down = lax.all_gather(adapter_down_factor[0], "tp", axis=0, tiled=True)
    kg, vg, back, qg4, hid4, wg = first_call(
        saved_queries[0],
        saved_keys[0],
        values[0],
        attention_output_grad[0],
        segments[:, None],
        segments[None, :],
        adapter_up_factor[0],
        hidden[0],
        shared_query_weight,
    )
    group = lax.dynamic_slice_in_dim(section_block_index[:, 0], y * 4, 4)
    ids = jnp.concatenate([group, c[None].astype(group.dtype)])
    partial = input_grad_call(ids, qg4, wg)
    summed = lax.psum_scatter(
        partial.reshape(NTP * 160, 2 * COLS), "tp", scatter_dimension=0, tiled=True
    ).reshape(5, 32, 2 * COLS)

    start = 896 * lo + 384 * c
    emb = jnp.stack(
        [lax.dynamic_slice_in_dim(embedding, start + 1792 * part, WIN, 1) for part in range(2)]
    )
    dw = weight_grad_call(ids, qg4, hid4, emb)
    back_rank = back.reshape(TOKENS, RANK)
    adapter = dot_nt(lax.dynamic_index_in_dim(back, t, keepdims=False), down)
    base = residual[0].astype(F32) + adapter[:, :WIDTH]
    adapter_embed = jnp.transpose(adapter[:, WIDTH:].reshape(32, NSEC, HD), (1, 0, 2))
    weight_grad, embed_part, next_base = second_call(dw, adapter_embed, base)

    qg = lax.dynamic_index_in_dim(qg4, j, keepdims=False)
    low_rank = (
        dot_nn(hidden[0], down[:WIDTH]) + dot_nn(embedding, down[WIDTH:])
    ).astype(BF16)
    up_grad = dot_tn(low_rank, qg)
    hidden_cols = lax.dynamic_slice_in_dim(hidden[0], (t % 8) * COLS, COLS, 1)
    embed_cols = lax.dynamic_slice_in_dim(embedding, (t % 8) * COLS, COLS, 1)
    down_grad = dot_tn(jnp.where(t < 8, hidden_cols, embed_cols), back_rank)

    emb_out = jnp.transpose(summed[4].reshape(32, 4, HD), (1, 0, 2))
    pland, eland = third_call(summed[:4], emb_out)
    moved = jnp.transpose(pland.reshape(4, 32, 2, COLS), (1, 2, 0, 3)).reshape(32, WIDTH)
    passed = jnp.where(s == NSEC - 1, 0.0, next_base + moved.astype(F32)).astype(BF16)
    embed_grad = embed_part + jnp.sum(eland.astype(F32), axis=0)
    return (
        kg[None],
        vg[None],
        down_grad[None],
        up_grad[None],
        weight_grad,
        passed[None],
        embed_grad,
    )


def solution(mesh):
    in_specs = (
        P("section", None, "tp"),
        P("section", None, "tp"),
        P("section", None, "tp"),
        P("section", None, "tp"),
        P(),
        P("section", None, None),
        P(),
        P(),
        P(None, "section", "tp"),
        P("section", "tp", None),
        P("section", None, "tp"),
        P("section", "tp", None),
    )
    out_specs = (
        P("section", None, "tp"),
        P("section", None, "tp"),
        P("section", "tp", None),
        P("section", None, "tp"),
        P(None, "section", "tp"),
        P("section", "tp", None),
        P("tp", "section"),
    )
    return jax.shard_map(
        on_device, mesh=mesh, in_specs=in_specs, out_specs=out_specs, check_vma=False
    )
```

time: 555 us -> 342 us (0.62)
  waiting for transfers between devices: 361 us -> 124 us
  Pallas kernels: 0 us -> 161 us
  blocking collectives: 74.6 us -> 0 us
  matrix products: 38.5 us -> 12.5 us
  other arithmetic: 22.3 us -> 4.73 us
  local copies, waits for them, and re-layouts: 33.7 us -> 24.2 us
  starting transfers between devices: 6.64 us -> 0.08 us
    pallas_call x0 -> x5, Pallas kernels: none -> 161 us  [the longest x1 74.6 us: first_call(): pl.pallas_call(first_kernel, out_shape=(jax.ShapeDtypeStruct((TOKENS, COL...]
    unnamed x6 -> x2, waiting for transfers between devices: 137 us -> 0.7 us
    reduce_scatter x1, waiting for transfers between devices: 222 us -> 123 us  [on_device(): lax.psum_scatter(partial.reshape(NTP * 160, 2 * COLS), 'tp', scatter_dime...]
    psum x1 -> x0, blocking collectives: 74.6 us -> none  [on_device(): returned_rank = lax.psum(returned_piece, 'tp').astype(jnp.bfloat16)]
    dot_general x12 -> x4, matrix products: 35.2 us -> 12.5 us  [the longest x2 7.32 us: dot_tn(): lax.dot_general(a, b, (((0,), (0,)), ((), ())), preferred_element_type=F32)]
    unnamed x34 -> x30, local copies, waits for them, and re-layouts: 26.7 us -> 13 us
    convert_element_type x3 -> x0, other arithmetic: 9.45 us -> none  [the longest x1 9.33 us: on_device(): partial_gradient.astype(jnp.bfloat16)]
    another operation x1, other arithmetic: 8.76 us -> 1.06 us  [on_device(): jnp.stack([lax.dynamic_slice_in_dim(embedding, start + 1792 * part, WIN,...]
  transfers between devices with their start and end apart: 5 -> 2, of which waited for: 4 -> 1; matrix products, arithmetic and copies ran while one was open for 16% -> 9% of each run, Pallas kernels for 0% -> 44%
where the time goes in v1:
time: 342 us; the launch traced here: 341 us
  Pallas kernels  161 us (47%)
  waiting for transfers between devices  124 us (36%)
  local copies, waits for them, and re-layouts  24.2 us (7%)
  between operations  14.3 us (4%)
  matrix products  12.5 us (4%)
  other arithmetic  4.73 us (1%)
    reduce_scatter x1, waiting for transfers between devices, on_device(): lax.psum_scatter(partial.reshape(NTP * 160, 2 * COLS), 'tp', scatter_dime...  123 us
    pallas_call x1, Pallas kernels, first_call(): pl.pallas_call(first_kernel, out_shape=(jax.ShapeDtypeStruct((TOKENS, COL...  74.6 us
    pallas_call x1, Pallas kernels, second_call(): pl.pallas_call(second_kernel, out_shape=(jax.ShapeDtypeStruct((2, COLS, C...  54.3 us
    unnamed x30, local copies, waits for them, and re-layouts  13 us
    pallas_call x1, Pallas kernels, third_call(): pl.pallas_call(third_kernel, out_shape=(jax.ShapeDtypeStruct((4, 32, 2 *...  13 us
    pallas_call x1, Pallas kernels, weight_grad_call(): pl.pallas_call(weight_grad_kernel, grid_spec=pltpu.PrefetchScalarGridSpec...  10 us
    pallas_call x1, Pallas kernels, input_grad_call(): pl.pallas_call(input_grad_kernel, grid_spec=pltpu.PrefetchScalarGridSpec(...  9.57 us
    dot_general x2, matrix products, dot_tn(): lax.dot_general(a, b, (((0,), (0,)), ((), ())), preferred_element_type=F32)  7.32 us
  transfers between devices with their start and end apart: 2, of which 1 were waited for; matrix products, arithmetic and copies ran while one was open for 9% of the time, Pallas kernels for 44%

profile of v1, /device:TPU:1, one launch (start us, length us, event | category | flops | bytes accessed | tf_op | source)
XLA Modules:
  0.0 340.9 jit_solution(13190903945325359059)
XLA Ops:
  7.2 0.0 copy-start
  7.2 0.0 copy-start.10
  7.2 0.0 copy-start.8
  7.2 0.0 all-gather.3.cloned.1.call-start
  7.2 0.7 all-gather.3.cloned.1.call-update
  7.9 0.0 reduce-scatter.2.cloned.1.call-start
  8.0 2.0 copy.27
  10.0 2.0 copy.28
  12.1 2.0 copy.29
  14.1 2.0 copy.30
  16.1 0.0 copy-done.10
  16.1 0.9 copy.32.segc_ref
  17.0 0.0 copy-done.8
  17.0 0.8 copy.31
  17.8 74.6 %attention_and_exchange.1 = (bf16[512,448]{1,0:T(8,128)(2,1)}, bf16[512,448]{1,0:T(8,128)(2,1)}, bf16[16,32,128]{2,1,0:T(8,128)(2,1)}, bf16[4,512,448]{2,1,0:T(8...) custom-call(bf16[512,448]{1,0:T(8,128)(2,1)} %bitcast.64, bf16[512,448]{1,0:T(8,128)(2,1)} %bitcast.65, ...), custom_call_target="tpu_custom_call" | custom-call | tf_op jit(solution)/shard_map/attention_and_exchange/pallas_call | solution.py:242
  92.4 0.0 copy-done
  92.4 0.1 fusion.15
  92.5 0.6 pad_add_fusion.ids
  93.1 9.6 %input_grad.1 = bf16[16,5,32,896]{3,2,1,0:T(8,128)(2,1)} custom-call(s32[5]{0:T(128)} %pad_add_fusion.ids, bf16[4,512,448]{2,1,0:T(8,128)(2,1)} %get-tuple-element.21.qg4_ref, bf16[2,1792,448]{2,1,0:T(8,128)(2,1)} %get-tuple-element.25.wh_ref.we_ref, bf16[2,1792,448]{2,1,0:T(8,128)(2,1)} %get-tuple-element.25.wh_ref.we_ref), custom_call_target="tpu_custom_call" | custom-call | flops 2466250752 | bytes 12582912 | tf_op jit(solution)/shard_map/input_grad/pallas_call | solution.py:292
  102.6 0.0 copy-start.4
  102.6 0.0 copy-start.3
  102.6 0.0 reduce-scatter.2.cloned.1.call-update
  102.7 0.0 copy-start.7
  102.7 0.9 copy-done.4
  103.7 1.0 copy.36
  104.6 0.0 copy-done.3
  104.6 1.0 copy.37
  105.6 1.3 dynamic-slice_bitcast_fusion.1
  106.9 1.1 pad_maximum_fusion.emb_ref
  107.9 0.0 copy-done.7
  108.0 2.7 convolution_bitcast_fusion.1
  110.7 0.0 copy-start.6
  110.7 10.0 %weight_grad.1.dw = bf16[4,2,448,448]{3,2,1,0:T(8,128)(2,1)} custom-call(s32[5]{0:T(128)} %pad_add_fusion.ids, bf16[4,512,448]{2,1,0:T(8,128)(2,1)} %get-tuple-element.21.qg4_ref, bf16[4,2,512,512]{3,2,1,0:T(8,128)(2,1)} %get-tuple-element.22.hid_ref, bf16[2,512,512]{2,1,0:T(8,128)(2,1)} %pad_maximum_fusion.emb_ref), custom_call_target="tpu_custom_call" | custom-call | flops 2818572288 | bytes 12582912 | tf_op jit(solution)/shard_map/weight_grad/pallas_call | solution.py:340
  120.7 0.0 all-gather.3.cloned.1.call-done
  120.7 2.2 fusion
  122.9 0.0 copy-done.6
  122.9 0.9 slice_add_fusion
  123.8 1.1 reshape.38
  124.9 0.0 copy-start.1
  124.9 2.3 copy.40
  127.2 54.3 %weight_sum.1 = (f32[2,448,448]{2,1,0:T(8,128)}, f32[32,224]{1,0:T(8,128)}, f32[32,3584]{1,0:T(8,128)}) custom-call(bf16[4,2,448,448]{3,2,1,0:T(8,128)(2,1)} %weight_grad.1.dw, f32[16,32,224]{2,1,0:T(8,128)} %bitcast.62, f32[32,3584]{1,0:T(8,128)} %get-tuple-element.45.base), custom_call_target="tpu_custom_call" | custom-call | flops 1000000000 | bytes 104857600 | tf_op jit(solution)/shard_map/weight_sum/pallas_call | solution.py:408
  181.5 0.0 copy-done.1
  181.6 3.0 fusion.3
  184.6 0.0 copy-start.9
  184.6 0.0 copy-start.5
  184.6 4.6 %convolution_bitcast_fusion = f32[1,128,448]{1,2,0:T(8,128)} fusion(f32[512,128]{1,0:T(8,128)} %fusion.3, bf16[512,3584]{1,0:T(8,128)(2,1)} %param.18, bf16[1,7168,128]{2,1,0:T(8,128)(2,1)} %all-gather.3.cloned.1.call-done, bf16[4,512,448]{2,1,0:T(8,128)(2,1)} %get-tuple-element.21.qg4_ref, s32[]{:T(128)S(6)} %select_n.66), kind=kOutput, calls=%fused_computation.3 | convolution fusion | flops 528613376 | bytes 5603332 | tf_op jit(solution)/shard_map/dot_general | solution.py:30
  189.2 0.0 copy-start.2
  189.2 123.0 %reduce-scatter.2.cloned.1.call-done = bf16[160,896]{1,0:T(8,128)(2,1)} async-done(((bf16[2560,896]{1,0:T(8,128)(2,1)}), bf16[160,896]{1,0:T(8,128)(2,1)}) %reduce-scatter.2.cloned.1.call-update) | async-done | bytes 286736 | tf_op jit(solution)/shard_map/reduce_scatter | solution.py:537
  312.2 0.8 slice.36
  313.0 0.1 reshape_squeeze.3
  313.1 0.6 copy.41
  313.7 1.6 slice.35
  315.4 13.0 %final_exchange.1 = (bf16[4,32,896]{2,1,0:T(8,128)(2,1)}, bf16[4,32,224]{2,1,0:T(8,128)(2,1)}) custom-call(bf16[4,32,896]{2,1,0:T(8,128)(2,1)} %bitcast.68, bf16[4,32,224]{2,1,0:T(8,128)(2,1)} %bitcast.72), custom_call_target="tpu_custom_call" | custom-call | tf_op jit(solution)/shard_map/final_exchange/pallas_call | solution.py:488
  328.4 0.9 convert_reduce_fusion
  329.2 1.5 reshape.42
  330.7 0.3 copy.35
  331.0 0.5 reshape.41
  331.5 0.0 copy-done.9
  331.5 0.6 add.70
  332.1 0.0 copy-done.5
  332.1 0.7 fusion.9
  332.9 0.0 copy-done.2
  332.9 1.2 copy.43
Async XLA Ops:
  7.2 85.2 %copy-start = (s32[16,1]{0,1:T(1,128)S(1)}, s32[16,1]{0,1:T(1,128)}, u32[]{:S(2)}) copy-start(s32[16,1]{0,1:T(1,128)} %param.19) | copy-start | bytes 196
  7.2 9.0 %copy-start.10 = (s32[512]{0:T(512)S(1)}, s32[512]{0:T(512)}, u32[]{:S(2)}) copy-start(s32[512]{0:T(512)} %param.16) | copy-start | bytes 6148
  7.2 9.8 %copy-start.8 = (bf16[1,128,448]{1,2,0:T(8,128)(2,1)S(1)}, bf16[1,128,448]{1,2,0:T(8,128)(2,1)}, u32[]{:S(2)}) copy-start(bf16[1,128,448]{1,2,0:T(8,128)(2,1)} %param.22) | copy-start | bytes 344068
  7.2 113.5 %all-gather.3.cloned.1.call-start = ((), (), s32[]{:S(2)}) async-start(), calls=%async_computation.2 | async-start | bytes 1949696 | tf_op jit(solution)/shard_map/all_gather | solution.py:522
  7.9 304.2 %reduce-scatter.2.cloned.1.call-start = ((), (), s32[]{:S(2)}) async-start(), calls=%async_computation.1 | async-start | bytes 4874240 | tf_op jit(solution)/shard_map/reduce_scatter | solution.py:537
  102.6 1.0 copy-start.4
  102.6 2.0 copy-start.3
  102.7 5.3 %copy-start.7 = (bf16[16,32,128]{2,1,0:T(8,128)(2,1)S(1)}, bf16[16,32,128]{2,1,0:T(8,128)(2,1)}, u32[]{:S(2)}) copy-start(bf16[16,32,128]{2,1,0:T(8,128)(2,1)} %get-tuple-element.20) | copy-start | bytes 393220
  110.7 12.2 %copy-start.6 = (bf16[1,32,3584]{2,1,0:T(8,128)(2,1)S(1)}, bf16[1,32,3584]{2,1,0:T(8,128)(2,1)}, u32[]{:S(2)}) copy-start(bf16[1,32,3584]{2,1,0:T(8,128)(2,1)} %param.23) | copy-start | bytes 688132
  124.9 56.6 %copy-start.1 = (bf16[1,512,3584]{2,1,0:T(8,128)(2,1)S(1)}, bf16[1,512,3584]{2,1,0:T(8,128)(2,1)}, u32[]{:S(2)}) copy-start(bf16[1,512,3584]{2,1,0:T(8,128)(2,1)} %param.17) | copy-start | bytes 11010052
  184.6 147.0 %copy-start.9 = (f32[32,224]{1,0:T(8,128)S(1)}, f32[32,224]{1,0:T(8,128)}, u32[]{:S(2)}) copy-start(f32[32,224]{1,0:T(8,128)} %get-tuple-element.27) | copy-start | bytes 86020
  184.6 147.6 %copy-start.5 = (f32[32,3584]{1,0:T(8,128)S(1)}, f32[32,3584]{1,0:T(8,128)}, u32[]{:S(2)}) copy-start(f32[32,3584]{1,0:T(8,128)} %get-tuple-element.24) | copy-start | bytes 1376260
  189.2 143.7 %copy-start.2 = (f32[2,448,448]{2,1,0:T(8,128)S(1)}, f32[2,448,448]{2,1,0:T(8,128)}, u32[]{:S(2)}) copy-start(f32[2,448,448]{2,1,0:T(8,128)} %get-tuple-element.58) | copy-start | bytes 4816900
Sparse Core Ops, SparseCore 0:
  10.6 86.1 all-gather.2
  102.8 209.3 reduce-scatter.1

commit v2 on v0

v2 whole, which is shorter than its diff:
```python
import jax
import jax.numpy as jnp
from jax import lax
from jax.experimental import pallas as pl
from jax.experimental.pallas import tpu as pltpu
from jax.sharding import PartitionSpec as P

MESH = pl.DeviceIdType.MESH
TOKENS = 512
WIDTH = 3584
COLS = 448
HD = 224
RANK = 128
WIN = 512
NSEC = 16
NTP = 16
SPLIT = 128
STEPS = 7
PARTS = 5
VMEM_LIMIT = 60 * 1024 * 1024
F32 = jnp.float32
BF16 = jnp.bfloat16


def dot_nt(a, b):
    return lax.dot_general(a, b, (((1,), (1,)), ((), ())), preferred_element_type=F32)


def dot_tn(a, b):
    return lax.dot_general(a, b, (((0,), (0,)), ((), ())), preferred_element_type=F32)


def dot_nn(a, b):
    return lax.dot_general(a, b, (((1,), (0,)), ((), ())), preferred_element_type=F32)


def remote(src, dst, send_sem, recv_sem, section, tp):
    return pltpu.make_async_remote_copy(
        src_ref=src,
        dst_ref=dst,
        send_sem=send_sem,
        recv_sem=recv_sem,
        device_id={"section": section, "tp": tp},
        device_id_type=MESH,
    )


def greet(peers):
    barrier = pltpu.get_barrier_semaphore()
    for section, tp in peers:
        pl.semaphore_signal(
            barrier, inc=1, device_id={"section": section, "tp": tp}, device_id_type=MESH
        )
    pl.semaphore_wait(barrier, len(peers))


def attention(q_ref, k_ref, v_ref, g_ref, seg_ref, qg, qgt, kg_ref, vg_ref):
    scale = HD ** (-0.5)
    seg_col = jnp.transpose(jnp.broadcast_to(seg_ref[...], (RANK, TOKENS)))[:, 0:1]
    key_id = lax.broadcasted_iota(jnp.int32, (TOKENS, TOKENS), 0)
    query_id = lax.broadcasted_iota(jnp.int32, (TOKENS, TOKENS), 1)
    allowed = (key_id <= query_id) & (seg_col == seg_ref[...])
    for head in range(2):
        rows = pl.ds(head * HD, HD)
        q, k, v, g = q_ref[rows, :], k_ref[rows, :], v_ref[rows, :], g_ref[rows, :]
        scores = jnp.where(allowed, dot_tn(k, q) * scale, -1e30)
        expo = jnp.exp(scores - jnp.max(scores, axis=0, keepdims=True))
        probs = expo / jnp.sum(expo, axis=0, keepdims=True)
        low = probs.astype(BF16)
        grad = dot_tn(v, g)
        delta = jnp.sum(low.astype(F32) * grad, axis=0, keepdims=True)
        dscore = (probs * (grad - delta)).astype(BF16)
        dq = (dot_nn(k, dscore) * scale).astype(BF16)
        qgt[rows, :] = dq
        qg[:, rows] = jnp.transpose(dq)
        kg_ref[rows, :] = (dot_nt(q, dscore) * scale).astype(BF16)
        vg_ref[rows, :] = dot_nt(g, low).astype(BF16)


def whole_kernel(
    ids, q_ref, k_ref, v_ref, g_ref, seg_ref, upt_ref, down_ref, hidden, embedding, weight, residual,
    kg_ref, vg_ref, dg_ref, ugt_ref, wsum_ref, pland, eland, next_res,
    qg, qgt, qg4, hid4, wg, embw, jw, adp, adw, bgrp, bpart, bland, bown, ball,
    partial, ring, hland, total, etotal, fbuf, qb, acc, dws, dwl,
    loc_sem, ws_sem, wr_sem, hs_sem, hr_sem, qs_sem, qr_sem, bs_sem, br_sem, cs_sem, cr_sem,
    ds_sem, dr_sem, gs_sem, gr_sem, rs_sem, rr_sem, is_sem, ir_sem, xs_sem, xr_sem,
    ps_sem, pr_sem, es_sem, er_sem, fin_sem, res_sem,
):
    s = lax.axis_index("section")
    t = lax.axis_index("tp")
    y, j = s // 4, s % 4
    lo, c = j // 2, j % 2
    hi, z = t // 8, t % 8
    sib = y * 4 + 2 * lo + (1 - c)
    across = [y * 4 + 2 * (1 - lo) + i for i in range(2)]
    partner = y * 4 + 2 * (1 - lo) + c
    t_far = (1 - hi) * 8 + z
    yl, yr, yo = (y + 3) % 4, (y + 1) % 4, (y + 2) % 4
    left, right = yl * 4 + j, yr * 4 + j
    z_next, z_prev = hi * 8 + (z + 1) % 8, hi * 8 + (z + 7) % 8
    tp_peers = [(t + i) % NTP for i in range(1, NTP)]
    section_peers = [(s + i) % NSEC for i in range(1, NSEC)]
    greet(
        [(p, t) for p in section_peers]
        + [(s, p) for p in tp_peers]
        + [(a, t_far) for a in across]
    )

    def row_block(b, owner_y):
        return wg.at[b, pl.ds(pl.multiple_of(owner_y * COLS, 64), COLS), :]

    def window(lo_d, c_d, part):
        return pl.ds(pl.multiple_of(896 * lo_d + 384 * c_d + 1792 * part, 128), WIN)

    wsends = []
    for n, (b, dest, slot) in enumerate([(0, right, 0), (1, left, 3), (1, right, 1), (0, left, 2)]):
        copy = remote(weight.at[b], row_block(b, y), ws_sem.at[n], wr_sem.at[slot], dest, t)
        copy.start()
        wsends.append(copy)

    hsends = []

    def send_hidden(part):
        for i in range(2):
            near = remote(
                hidden.at[pl.ds(0, SPLIT), window(1 - lo, i, part)],
                hid4.at[j, part, pl.ds(0, SPLIT), :],
                hs_sem.at[len(hsends)], hr_sem.at[2 + 2 * c + part], across[i], t,
            )
            near.start()
            hsends.append(near)
            far = remote(
                hidden.at[pl.ds(SPLIT, TOKENS - SPLIT), window(1 - lo, i, part)],
                hid4.at[j, part, pl.ds(SPLIT, TOKENS - SPLIT), :],
                hs_sem.at[len(hsends)], hr_sem.at[6 + 2 * c + part], across[i], t_far,
            )
            far.start()
            hsends.append(far)
        twin = remote(
            hidden.at[:, window(lo, 1 - c, part)], hid4.at[j, part],
            hs_sem.at[len(hsends)], hr_sem.at[part], sib, t,
        )
        twin.start()
        hsends.append(twin)

    locals_ = []

    def here(src, dst):
        copy = pltpu.make_async_copy(src, dst, loc_sem.at[len(locals_)])
        copy.start()
        locals_.append(copy)
        return copy

    jwin = pl.ds(pl.multiple_of(896 * (z // 2) + 384 * (z % 2), 128), WIN)
    from_hidden = pltpu.make_async_copy(hidden.at[:, jwin], jw, loc_sem.at[8])
    from_embedding = pltpu.make_async_copy(embedding.at[:, jwin], jw, loc_sem.at[8])

    @pl.when(t < 8)
    def _():
        from_hidden.start()

    @pl.when(t >= 8)
    def _():
        from_embedding.start()

    send_hidden(0)
    for b in range(2):
        here(weight.at[b], row_block(b, y))
    for part in range(2):
        here(hidden.at[:, window(lo, c, part)], hid4.at[j, part])
        here(embedding.at[:, window(lo, c, part)], embw.at[part])

    adder = t % 4
    half = (t // 4) % 2
    mine = pl.ds(pl.multiple_of(half * COLS, 64), COLS)
    other = pl.ds(pl.multiple_of((1 - half) * COLS, 64), COLS)
    down_copy = remote(down_ref, adw.at[j, mine, :], gs_sem.at[0], gr_sem.at[j], y * 4 + adder, t)
    back_copy = remote(
        ball.at[:, :, pl.ds(0, RANK)], bgrp.at[j], gs_sem.at[1], gr_sem.at[4 + j], y * 4 + adder, t
    )
    adw[:, other, :] = jnp.zeros((4, COLS, RANK), BF16)

    @pl.when(j != adder)
    def _():
        down_copy.start()

    @pl.when(j == adder)
    def _():
        adw[j, mine, :] = down_ref[...]

    res_copy = remote(
        residual, next_res, res_sem.at[0], res_sem.at[1], (s + NSEC - 1) % NSEC, t
    )
    res_copy.start()

    attention(q_ref, k_ref, v_ref, g_ref, seg_ref, qg, qgt, kg_ref, vg_ref)

    q_near = remote(qg, qg4.at[j], qs_sem.at[0], qr_sem.at[j], partner, t)
    q_near.start()
    q_twin = remote(qg, qg4.at[j], qs_sem.at[1], qr_sem.at[j], sib, t)
    q_twin.start()
    qg4[j] = qg[...]

    adp[...] = jnp.zeros_like(adp)
    adp[pl.ds(pl.multiple_of(64 * (z % 2), 64), COLS), :] = down_ref[...]
    bpart[:, :, 0:RANK] = dot_nn(qg[...], upt_ref[...]).reshape(NTP, 32, RANK)
    from_hidden.wait()
    bpart[:, :, RANK : 2 * RANK] = dot_nn(jw[...], adp[...]).reshape(NTP, 32, RANK)
    bsends = []
    for n, peer in enumerate(tp_peers):
        copy = remote(bpart.at[peer], bland.at[t], bs_sem.at[n], br_sem.at[t], s, peer)
        copy.start()
        bsends.append(copy)
    bland[t] = bpart[t]
    send_hidden(1)

    def wait_w(b, owner_y, slot):
        remote(weight.at[b], row_block(b, owner_y), ws_sem.at[0], wr_sem.at[slot], left, t).wait_recv()

    wait_w(0, yl, 0)
    copy = remote(row_block(0, yl), row_block(0, yl), ws_sem.at[4], wr_sem.at[4], right, t)
    copy.start()
    wsends.append(copy)
    wait_w(1, yr, 3)
    copy = remote(row_block(1, yr), row_block(1, yr), ws_sem.at[5], wr_sem.at[5], left, t)
    copy.start()
    wsends.append(copy)

    for peer in tp_peers:
        remote(bpart.at[peer], bland.at[peer], bs_sem.at[0], br_sem.at[peer], s, peer).wait_recv()
    bown[...] = jnp.sum(bland[...], axis=0).astype(BF16)
    csends = []
    for n, peer in enumerate(tp_peers):
        copy = remote(bown, ball.at[t], cs_sem.at[n], cr_sem.at[t], s, peer)
        copy.start()
        csends.append(copy)
    ball[t] = bown[...]

    def wait_q(slot):
        remote(qg, qg4.at[slot], qs_sem.at[0], qr_sem.at[slot], sib, t).wait_recv()

    slot_partner = 2 * (1 - lo) + c
    wait_q(slot_partner)
    q_on = remote(
        qg4.at[slot_partner], qg4.at[slot_partner], qs_sem.at[2], qr_sem.at[slot_partner], sib, t
    )
    q_on.start()

    for peer in tp_peers:
        remote(bown, ball.at[peer], cs_sem.at[0], cr_sem.at[peer], s, peer).wait_recv()

    @pl.when(j != adder)
    def _():
        back_copy.start()

    @pl.when(j == adder)
    def _():
        bgrp[j] = ball[:, :, 0:RANK]

    wait_q(2 * lo + 1 - c)
    wait_q(2 * (1 - lo) + 1 - c)

    def keep(n, b):
        return jnp.where(ids[4 * y + n] == b, 1.0, 0.0).astype(F32)

    for b in range(2):
        picked = qg4[0].astype(F32) * keep(0, b)
        for n in range(1, 4):
            picked = picked + qg4[n].astype(F32) * keep(n, b)
        qb[b] = picked.astype(BF16)

    @pl.when(j == adder)
    def _():
        for n in range(4):
            @pl.when(j != n)
            def _():
                remote(
                    down_ref, adw.at[n, mine, :], gs_sem.at[0], gr_sem.at[n], y * 4 + adder, t
                ).wait_recv()
                remote(
                    ball.at[:, :, pl.ds(0, RANK)], bgrp.at[n], gs_sem.at[1], gr_sem.at[4 + n], y * 4 + adder, t
                ).wait_recv()

    for copy in locals_:
        copy.wait()
    wait_w(1, yl, 1)
    wait_w(0, yr, 2)
    wait_w(0, yo, 4)
    wait_w(1, yo, 5)

    def chunk(d, k):
        return (z + 15 - k) % 8 if d == 0 else 8 + (z + 1 + k) % 8

    def hop(d, p, k):
        return remote(
            partial.at[chunk(d, k), p], ring.at[d, p, k],
            rs_sem.at[d, p, k], rr_sem.at[d, p, k], s, z_next if d == 0 else z_prev,
        )

    for p in range(PARTS):
        if p < 4:
            picked = wg[0, 0 : 2 * COLS, :] * keep(p, 0).astype(BF16) + wg[
                1, 0 : 2 * COLS, :
            ] * keep(p, 1).astype(BF16)
            fbuf[...] = dot_nt(qg4[p], picked)

            @pl.when((j == adder) & (t < 8))
            def _():
                fbuf[...] += dot_nt(bgrp[p].reshape(TOKENS, RANK), adw[p])
        else:
            fbuf[...] = dot_nt(qb[0], wg[0, 2 * COLS :, :]) + dot_nt(qb[1], wg[1, 2 * COLS :, :])

            @pl.when((j == adder) & (t >= 8))
            def _():
                for n in range(4):
                    fbuf[...] += dot_nt(bgrp[n].reshape(TOKENS, RANK), adw[n])

        partial[:, p] = fbuf[...].reshape(NTP, 32, 2 * COLS).astype(BF16)
        for d in range(2):
            hop(d, p, 0).start()

    for part in range(2):
        remote(
            hidden.at[:, window(lo, c, part)], hid4.at[2 * lo + 1 - c, part],
            hs_sem.at[0], hr_sem.at[part], sib, t,
        ).wait_recv()
        for i in range(2):
            for first, count, base in ((0, SPLIT, 2), (SPLIT, TOKENS - SPLIT, 6)):
                remote(
                    hidden.at[pl.ds(first, count), window(lo, c, part)],
                    hid4.at[2 * (1 - lo) + i, part, pl.ds(first, count), :],
                    hs_sem.at[0], hr_sem.at[base + 2 * i + part], sib, t,
                ).wait_recv()

    skip = pl.ds(pl.multiple_of(64 * c, 64), COLS)

    def weight_send(i, yd):
        return remote(dws.at[i], dwl.at[i], xs_sem.at[i], xr_sem.at[i], yd * 4 + j, t)

    def ring_step(k, carry):
        for p in range(PARTS):
            for d in range(2):
                hop(d, p, k - 1).wait_recv()
                partial[chunk(d, k), p] = (
                    partial[chunk(d, k), p].astype(F32) + ring[d, p, k - 1].astype(F32)
                ).astype(BF16)
                hop(d, p, k).start()

        @pl.when(k <= 4)
        def _():
            yd = (y + k) % 4

            @pl.when(yd < 2)
            def _():
                for n in range(4):
                    term = dot_tn(hid4[n, yd], qg4[n])
                    for b in range(2):
                        if n == 0:
                            acc[b] = term * keep(n, b)
                        else:
                            acc[b] += term * keep(n, b)

            @pl.when(yd >= 2)
            def _():
                for b in range(2):
                    acc[b] = dot_tn(embw[yd % 2], qb[b])

            for b in range(2):
                dws[k - 1, b] = acc[b, skip, :].astype(BF16)

            @pl.when(k < 4)
            def _():
                weight_send(k - 1, yd).start()

        return carry

    lax.fori_loop(1, STEPS, ring_step, 0)

    back = ball[:, :, 0:RANK].reshape(TOKENS, RANK)
    low = ball[:, :, RANK : 2 * RANK].reshape(TOKENS, RANK)
    ugt_ref[...] = dot_nn(qgt[...], low)
    fbuf[:, 0:RANK] = dot_tn(jw[...], back)
    dg_ref[...] = fbuf[pl.ds(pl.multiple_of(64 * (z % 2), 64), COLS), 0:RANK]

    def swap(p):
        return remote(
            partial.at[(1 - hi) * 8 + z, p], hland.at[p], is_sem.at[p], ir_sem.at[p], s, t_far
        )

    for p in range(PARTS):
        for d in range(2):
            hop(d, p, STEPS - 1).wait_recv()
            partial[chunk(d, STEPS), p] = (
                partial[chunk(d, STEPS), p].astype(F32) + ring[d, p, STEPS - 1].astype(F32)
            ).astype(BF16)
        swap(p).start()

    for i in range(3):
        weight_send(i, yl).wait_recv()
    for b in range(2):
        wsum_ref[b] = (
            dws[3, b].astype(F32) + dwl[0, b].astype(F32)
            + (dwl[1, b].astype(F32) + dwl[2, b].astype(F32))
        )

    def move(src, dst, send_sem, recv_sem, here_sem, dest):
        away = remote(src, dst, send_sem, recv_sem, dest, t)
        near = pltpu.make_async_copy(src, dst, here_sem)

        @pl.when(dest != s)
        def _():
            away.start()

        @pl.when(dest == s)
        def _():
            near.start()

        def finish():
            @pl.when(dest != s)
            def _():
                away.wait_send()

            @pl.when(dest == s)
            def _():
                near.wait()

        return finish

    ends = []
    for p in range(PARTS):
        swap(p).wait_recv()
        value = partial[hi * 8 + z, p].astype(F32) + hland[p].astype(F32)
        if p < 4:
            total[p] = value.astype(BF16)
            dest = (y * 4 + p + NSEC - 1) % NSEC
            ends.append(
                move(total.at[p], pland.at[j], ps_sem.at[p], pr_sem.at[j], fin_sem.at[p], dest)
            )
        else:
            for n in range(4):
                etotal[n] = value[:, n * HD : (n + 1) * HD]
                dest = 2 * j + n % 2 + 8 * (n // 2)
                ends.append(
                    move(etotal.at[n], eland.at[y], es_sem.at[n], er_sem.at[y], fin_sem.at[4 + n], dest)
                )

    for n in range(4):
        source = (((s + 1) % NSEC) // 4) * 4 + n

        @pl.when(source != s)
        def _():
            remote(total.at[n], pland.at[n], ps_sem.at[n], pr_sem.at[n], source, t).wait_recv()

    for n in range(4):
        source = n * 4 + (s % 8) // 2

        @pl.when(source != s)
        def _():
            remote(etotal.at[n], eland.at[n], es_sem.at[n], er_sem.at[n], source, t).wait_recv()

    for end in ends:
        end()
    res_copy.wait()
    for copy in wsends + hsends + bsends + csends + [q_near, q_twin, q_on]:
        copy.wait_send()

    @pl.when(j != adder)
    def _():
        down_copy.wait_send()
        back_copy.wait_send()

    def drain(k, carry):
        for p in range(PARTS):
            for d in range(2):
                hop(d, p, k).wait_send()
        return carry

    lax.fori_loop(0, STEPS, drain, 0)
    for p in range(PARTS):
        swap(p).wait_send()
    for i in range(3):
        weight_send(i, yl).wait_send()


def whole_call(ids, q, k, v, g, seg, upt, down, hidden, embedding, weight, residual):
    vm = pl.BlockSpec(memory_space=pltpu.VMEM)
    sm = pl.BlockSpec(memory_space=pltpu.SMEM)
    anys = pl.BlockSpec(memory_space=pl.ANY)
    dma = pltpu.SemaphoreType.DMA
    out = jax.ShapeDtypeStruct
    return pl.pallas_call(
        whole_kernel,
        out_shape=(
            out((COLS, TOKENS), BF16),
            out((COLS, TOKENS), BF16),
            out((COLS, RANK), F32),
            out((COLS, RANK), F32),
            out((2, COLS, COLS), F32),
            out((4, 32, 2 * COLS), BF16),
            out((4, 32, HD), F32),
            out((32, WIDTH), BF16),
        ),
        in_specs=[sm] + [vm] * 7 + [anys] * 4,
        out_specs=(vm, vm, vm, vm, vm, anys, anys, anys),
        scratch_shapes=[
            pltpu.VMEM((TOKENS, COLS), BF16),
            pltpu.VMEM((COLS, TOKENS), BF16),
            pltpu.VMEM((4, TOKENS, COLS), BF16),
            pltpu.VMEM((4, 2, TOKENS, WIN), BF16),
            pltpu.VMEM((2, 4 * COLS, COLS), BF16),
            pltpu.VMEM((2, TOKENS, WIN), BF16),
            pltpu.VMEM((TOKENS, WIN), BF16),
            pltpu.VMEM((WIN, RANK), BF16),
            pltpu.VMEM((4, 2 * COLS, RANK), BF16),
            pltpu.VMEM((4, NTP, 32, RANK), BF16),
            pltpu.VMEM((NTP, 32, 2 * RANK), F32),
            pltpu.VMEM((NTP, 32, 2 * RANK), F32),
            pltpu.VMEM((32, 2 * RANK), BF16),
            pltpu.VMEM((NTP, 32, 2 * RANK), BF16),
            pltpu.VMEM((NTP, PARTS, 32, 2 * COLS), BF16),
            pltpu.VMEM((2, PARTS, STEPS, 32, 2 * COLS), BF16),
            pltpu.VMEM((PARTS, 32, 2 * COLS), BF16),
            pltpu.VMEM((4, 32, 2 * COLS), BF16),
            pltpu.VMEM((4, 32, HD), F32),
            pltpu.VMEM((TOKENS, 2 * COLS), F32),
            pltpu.VMEM((2, TOKENS, COLS), BF16),
            pltpu.VMEM((2, WIN, COLS), F32),
            pltpu.VMEM((4, 2, COLS, COLS), BF16),
            pltpu.VMEM((3, 2, COLS, COLS), BF16),
            dma((9,)), dma((6,)), dma((6,)), dma((10,)), dma((10,)), dma((3,)), dma((4,)),
            dma((15,)), dma((16,)), dma((15,)), dma((16,)),
            dma((1,)), dma((1,)), dma((2,)), dma((8,)),
            dma((2, PARTS, STEPS)), dma((2, PARTS, STEPS)),
            dma((PARTS,)), dma((PARTS,)), dma((3,)), dma((3,)),
            dma((4,)), dma((4,)), dma((4,)), dma((4,)), dma((8,)), dma((2,)),
        ],
        compiler_params=pltpu.CompilerParams(
            collective_id=0, has_side_effects=True, vmem_limit_bytes=VMEM_LIMIT
        ),
        name="attention_block_backward",
    )(ids, q, k, v, g, seg, upt, down, hidden, embedding, weight, residual)


def on_device(
    saved_queries,
    saved_keys,
    values,
    attention_output_grad,
    segments,
    hidden,
    embedding,
    section_block_index,
    shared_query_weight,
    adapter_down_factor,
    adapter_up_factor,
    residual,
):
    s = lax.axis_index("section")
    kgt, vgt, down_grad, ugt, weight_grad, pland, eland, next_res = whole_call(
        section_block_index[:, 0],
        saved_queries[0].T,
        saved_keys[0].T,
        values[0].T,
        attention_output_grad[0].T,
        segments[None, :],
        adapter_up_factor[0].T,
        adapter_down_factor[0],
        hidden[0],
        embedding,
        shared_query_weight,
        residual[0],
    )
    moved = jnp.transpose(pland.reshape(4, 32, 2, COLS), (1, 2, 0, 3)).reshape(32, WIDTH)
    passed = jnp.where(
        s == NSEC - 1, 0.0, next_res.astype(F32) + moved.astype(F32)
    ).astype(BF16)
    return (
        kgt.T[None],
        vgt.T[None],
        down_grad[None],
        ugt.T[None],
        weight_grad,
        passed[None],
        jnp.sum(eland, axis=0),
    )


def solution(mesh):
    in_specs = (
        P("section", None, "tp"),
        P("section", None, "tp"),
        P("section", None, "tp"),
        P("section", None, "tp"),
        P(),
        P("section", None, None),
        P(),
        P(),
        P(None, "section", "tp"),
        P("section", "tp", None),
        P("section", None, "tp"),
        P("section", "tp", None),
    )
    out_specs = (
        P("section", None, "tp"),
        P("section", None, "tp"),
        P("section", "tp", None),
        P("section", None, "tp"),
        P(None, "section", "tp"),
        P("section", "tp", None),
        P("tp", "section"),
    )
    return jax.shard_map(
        on_device, mesh=mesh, in_specs=in_specs, out_specs=out_specs, check_vma=False
    )
```

time: 555 us -> 142 us (0.26)
  the two profiles are of different devices: /device:TPU:1 before, /device:TPU:25 now
where the time goes in v2:
time: 142 us
  Pallas kernels  129 us (91%)
  local copies, waits for them, and re-layouts  8.41 us (6%)
  other arithmetic  3.37 us (2%)
    pallas_call x1, Pallas kernels, whole_call(): pl.pallas_call(whole_kernel, out_shape=(out((COLS, TOKENS), BF16), out((C...  129 us
    unnamed x11, local copies, waits for them, and re-layouts  6.15 us

profile of v2, /device:TPU:25, one launch (start us, length us, event | category | flops | bytes accessed | tf_op | source)
XLA Modules:
  0.0 141.8 jit_solution(6865222442468762545)
XLA Ops:
  0.6 129.3 %attention_block_backward.1 = (bf16[448,512]{1,0:T(8,128)(2,1)}, bf16[448,512]{1,0:T(8,128)(2,1)}, f32[448,128]{1,0:T(8,128)}, f32[448,128]{1,0:T(8,128)}, f32[2...) custom-call(s32[16]{0:T(128)} %bitcast.49, ...), custom_call_target="tpu_custom_call" | custom-call | tf_op jit(solution)/shard_map/attention_block_backward/pallas_call | solution.py:491
  130.0 0.0 copy-start.1
  130.0 0.0 copy-start
  130.0 1.7 %reduce_sum.9 = f32[32,224]{1,0:T(8,128)} reduce(f32[4,32,224]{2,1,0:T(8,128)} %get-tuple-element.22, f32[]{:T(128)} %constant.8.clone.1), dimensions={0}, to_apply=%region_0.1 | reduce | flops 21504 | bytes 143364 | tf_op jit(solution)/shard_map/reduce_sum | solution.py:584
  131.7 1.4 %reshape.21 = f32[4,32,2,448]{3,2,1,0:T(2,128)S(1)} reshape(bf16[4,32,896]{2,1,0:T(8,128)(2,1)} %get-tuple-element.21) | data formatting | bytes 688128 | tf_op jit(solution)/shard_map/convert_element_type | solution.py:575
  133.1 0.3 copy.21
  133.5 0.0 copy-start.2
  133.5 0.5 reshape.20
  133.9 1.7 %fusion = bf16[1,32,3584]{2,1,0:T(8,128)(2,1)} fusion(f32[32,3584]{1,0:T(8,128)S(1)} %reshape.20, bf16[32,3584]{1,0:T(8,128)(2,1)} %get-tuple-element.20, pred[]{:T(512)S(6)} %eq.3), kind=kLoop, calls=%fused_computation.2 | loop fusion | flops 458752 | bytes 917505 | tf_op jit(solution)/shard_map/broadcast_in_dim | solution.py:583
  135.6 1.8 %copy.27 = bf16[1,512,448]{1,2,0:T(8,128)(2,1)} copy(bf16[1,512,448]{1,2,0:T(8,128)(2,1)} %bitcast.38) | data formatting | bytes 917504
  137.4 0.0 copy-done.1
  137.5 0.8 copy.28
  138.2 1.6 %copy.29 = f32[1,448,128]{2,1,0:T(8,128)} copy(f32[1,448,128]{2,1,0:T(8,128)} %bitcast.44) | data formatting | bytes 458752
  139.9 0.0 copy-done.2
  139.9 0.7 copy.30
  140.6 0.0 copy-done
  140.6 1.2 copy.31
Async XLA Ops:
  130.0 7.5 %copy-start.1 = (bf16[448,512]{1,0:T(8,128)(2,1)S(1)}, bf16[448,512]{1,0:T(8,128)(2,1)}, u32[]{:S(2)}) copy-start(bf16[448,512]{1,0:T(8,128)(2,1)} %get-tuple-element.16) | copy-start | bytes 1376260
  130.0 10.6 %copy-start = (f32[2,448,448]{2,1,0:T(8,128)S(1)}, f32[2,448,448]{2,1,0:T(8,128)}, u32[]{:S(2)}) copy-start(f32[2,448,448]{2,1,0:T(8,128)} %get-tuple-element.34) | copy-start | bytes 4816900
  133.5 6.4 %copy-start.2 = (f32[448,128]{1,0:T(8,128)S(1)}, f32[448,128]{1,0:T(8,128)}, u32[]{:S(2)}) copy-start(f32[448,128]{1,0:T(8,128)} %get-tuple-element.18) | copy-start | bytes 688132

commit v3 on v2

v3 whole, which is shorter than its diff:
```python
import jax
import jax.numpy as jnp
from jax import lax
from jax.experimental import pallas as pl
from jax.experimental.pallas import tpu as pltpu
from jax.sharding import PartitionSpec as P

MESH = pl.DeviceIdType.MESH
TOKENS = 512
WIDTH = 3584
COLS = 448
HD = 224
RANK = 128
WIN = 512
NSEC = 16
NTP = 16
SPLIT = 192
STEPS = 7
HALF = 224
PARTS = 5
VMEM_LIMIT = 60 * 1024 * 1024
F32 = jnp.float32
BF16 = jnp.bfloat16


def dot_nt(a, b):
    return lax.dot_general(a, b, (((1,), (1,)), ((), ())), preferred_element_type=F32)


def dot_tn(a, b):
    return lax.dot_general(a, b, (((0,), (0,)), ((), ())), preferred_element_type=F32)


def dot_nn(a, b):
    return lax.dot_general(a, b, (((1,), (0,)), ((), ())), preferred_element_type=F32)


def remote(src, dst, send_sem, recv_sem, section, tp):
    return pltpu.make_async_remote_copy(
        src_ref=src,
        dst_ref=dst,
        send_sem=send_sem,
        recv_sem=recv_sem,
        device_id={"section": section, "tp": tp},
        device_id_type=MESH,
    )


def greet(peers):
    barrier = pltpu.get_barrier_semaphore()
    for section, tp in peers:
        pl.semaphore_signal(
            barrier, inc=1, device_id={"section": section, "tp": tp}, device_id_type=MESH
        )
    pl.semaphore_wait(barrier, len(peers))


def attention(q_ref, k_ref, v_ref, g_ref, seg_ref, qg, qgt, kg_ref, vg_ref):
    scale = HD ** (-0.5)
    seg_col = jnp.transpose(jnp.broadcast_to(seg_ref[...], (RANK, TOKENS)))[:, 0:1]
    key_id = lax.broadcasted_iota(jnp.int32, (TOKENS, TOKENS), 0)
    query_id = lax.broadcasted_iota(jnp.int32, (TOKENS, TOKENS), 1)
    allowed = (key_id <= query_id) & (seg_col == seg_ref[...])
    for head in range(2):
        rows = pl.ds(head * HD, HD)
        q, k, v, g = q_ref[rows, :], k_ref[rows, :], v_ref[rows, :], g_ref[rows, :]
        scores = jnp.where(allowed, dot_tn(k, q) * scale, -1e30)
        expo = jnp.exp(scores - jnp.max(scores, axis=0, keepdims=True))
        probs = expo / jnp.sum(expo, axis=0, keepdims=True)
        low = probs.astype(BF16)
        grad = dot_tn(v, g)
        delta = jnp.sum(low.astype(F32) * grad, axis=0, keepdims=True)
        dscore = (probs * (grad - delta)).astype(BF16)
        dq = (dot_nn(k, dscore) * scale).astype(BF16)
        qgt[rows, :] = dq
        qg[:, rows] = jnp.transpose(dq)
        kg_ref[rows, :] = (dot_nt(q, dscore) * scale).astype(BF16)
        vg_ref[rows, :] = dot_nt(g, low).astype(BF16)


def whole_kernel(
    ids, q_ref, k_ref, v_ref, g_ref, seg_ref, upt_ref, down_ref, res_ref, hidden, embedding, weight,
    kg_ref, vg_ref, dg_ref, ugt_ref, wsum_ref, passed_ref, embed_ref,
    qg, qgt, qg4, hid4, wg, embw, jw, adp, dfull, bpart, bland, bown, ball,
    partial, ring, hland, total, etotal, pland, eland, nsend, nland, apsend, apland, fbuf, qb, acc, dws, dwl,
    loc_sem, ws_sem, wr_sem, hs_sem, hr_sem, qs_sem, qr_sem, bs_sem, br_sem, cs_sem, cr_sem,
    ds_sem, dr_sem, rs_sem, rr_sem, is_sem, ir_sem, xs_sem, xr_sem,
    ps_sem, pr_sem, es_sem, er_sem, fin_sem, ns_sem, as_sem, ar_sem,
):
    s = lax.axis_index("section")
    t = lax.axis_index("tp")
    y, j = s // 4, s % 4
    lo, c = j // 2, j % 2
    hi, z = t // 8, t % 8
    sib = y * 4 + 2 * lo + (1 - c)
    across = [y * 4 + 2 * (1 - lo) + i for i in range(2)]
    partner = y * 4 + 2 * (1 - lo) + c
    t_far = (1 - hi) * 8 + z
    yl, yr, yo = (y + 3) % 4, (y + 1) % 4, (y + 2) % 4
    left, right = yl * 4 + j, yr * 4 + j
    yin, yout = y + 1 - 2 * (y % 2), 3 - y
    z_next, z_prev = hi * 8 + (z + 1) % 8, hi * 8 + (z + 7) % 8
    tp_peers = [(t + i) % NTP for i in range(1, NTP)]
    section_peers = [(s + i) % NSEC for i in range(1, NSEC)]
    greet(
        [(p, t) for p in section_peers]
        + [(s, p) for p in tp_peers]
        + [(a, t_far) for a in across]
    )
    sent = []

    def go(copy):
        copy.start()
        sent.append(copy)
        return copy

    def piece(i, owner_y):
        first = pl.multiple_of(owner_y * COLS + HALF * (i % 2), 32)
        return wg.at[i // 2, pl.ds(first, HALF), :]

    def w_own(i, to_in):
        n = 4 * to_in + i
        return remote(
            weight.at[i // 2, pl.ds(HALF * (i % 2), HALF), :], piece(i, y),
            ws_sem.at[n], wr_sem.at[n], (yin if to_in else yout) * 4 + j, t,
        )

    def w_on(i):
        return remote(
            piece(i, yout), piece(i, yout), ws_sem.at[8 + i], wr_sem.at[8 + i], yin * 4 + j, t
        )

    def w_wait(kind, i):
        owner = (yout, yin, 3 - yin)[kind]
        n = 4 * kind + i
        remote(piece(i, owner), piece(i, owner), ws_sem.at[0], wr_sem.at[n], yin * 4 + j, t).wait_recv()

    @pl.when(y < 2)
    def _():
        for i in range(4):
            w_own(i, 1).start()

    for i in range(4):
        go(w_own(i, 0))

    def z_at(step):
        return (z + step + 8) % 8

    def d_send(n, slot, to):
        return remote(dfull.at[slot], dfull.at[slot], ds_sem.at[n], dr_sem.at[slot], s, to)

    def d_wait(slot):
        d_send(0, slot, t_far).wait_recv()

    dfull[t] = down_ref[...]
    for n, to in enumerate([t_far] + [hi * 8 + z_at(i) for i in (1, -1, 2, -2)]):
        go(d_send(n, t, to))

    def window(lo_d, c_d, part):
        return pl.ds(pl.multiple_of(896 * lo_d + 384 * c_d + 1792 * part, 128), WIN)

    def send_hidden(part):
        n = 5 * part
        for i in range(2):
            go(remote(
                hidden.at[pl.ds(0, SPLIT), window(1 - lo, i, part)],
                hid4.at[j, part, pl.ds(0, SPLIT), :],
                hs_sem.at[n + 2 * i], hr_sem.at[2 + 2 * c + part], across[i], t,
            ))
            go(remote(
                hidden.at[pl.ds(SPLIT, TOKENS - SPLIT), window(1 - lo, i, part)],
                hid4.at[j, part, pl.ds(SPLIT, TOKENS - SPLIT), :],
                hs_sem.at[n + 2 * i + 1], hr_sem.at[6 + 2 * c + part], across[i], t_far,
            ))
        go(remote(
            hidden.at[:, window(lo, 1 - c, part)], hid4.at[j, part],
            hs_sem.at[n + 4], hr_sem.at[part], sib, t,
        ))

    locals_ = []

    def here(src, dst):
        copy = pltpu.make_async_copy(src, dst, loc_sem.at[len(locals_)])
        copy.start()
        locals_.append(copy)

    jwin = pl.ds(pl.multiple_of(896 * (z // 2) + 384 * (z % 2), 128), WIN)
    from_hidden = pltpu.make_async_copy(hidden.at[:, jwin], jw, loc_sem.at[8])
    from_embedding = pltpu.make_async_copy(embedding.at[:, jwin], jw, loc_sem.at[8])

    @pl.when(t < 8)
    def _():
        from_hidden.start()

    @pl.when(t >= 8)
    def _():
        from_embedding.start()

    send_hidden(0)
    for b in range(2):
        here(weight.at[b], wg.at[b, pl.ds(pl.multiple_of(y * COLS, 64), COLS), :])
    for part in range(2):
        here(hidden.at[:, window(lo, c, part)], hid4.at[j, part])
        here(embedding.at[:, window(lo, c, part)], embw.at[part])

    attention(q_ref, k_ref, v_ref, g_ref, seg_ref, qg, qgt, kg_ref, vg_ref)

    go(remote(qg, qg4.at[j], qs_sem.at[0], qr_sem.at[j], partner, t))
    go(remote(qg, qg4.at[j], qs_sem.at[1], qr_sem.at[j], sib, t))
    qg4[j] = qg[...]

    w_wait(0, 0)
    go(w_on(0))

    d_wait(t_far)
    for n, to in enumerate([hi * 8 + z_at(i) for i in (1, -1, 2, -2)]):
        go(d_send(5 + n, t_far, to))

    adp[...] = jnp.zeros_like(adp)
    adp[pl.ds(pl.multiple_of(64 * (z % 2), 64), COLS), :] = down_ref[...]
    bpart[:, :, 0:RANK] = dot_nn(qg[...], upt_ref[...]).reshape(NTP, 32, RANK)
    from_hidden.wait()
    bpart[:, :, RANK : 2 * RANK] = dot_nn(jw[...], adp[...]).reshape(NTP, 32, RANK)
    for n, peer in enumerate(tp_peers):
        go(remote(bpart.at[peer], bland.at[t], bs_sem.at[n], br_sem.at[t], s, peer))
    bland[t] = bpart[t]

    w_wait(0, 1)
    go(w_on(1))
    send_hidden(1)

    def wait_q(slot):
        remote(qg, qg4.at[slot], qs_sem.at[0], qr_sem.at[slot], sib, t).wait_recv()

    w_wait(0, 2)
    go(w_on(2))
    slot_partner = 2 * (1 - lo) + c
    wait_q(slot_partner)
    go(remote(
        qg4.at[slot_partner], qg4.at[slot_partner], qs_sem.at[2], qr_sem.at[slot_partner], sib, t
    ))

    for m, other in enumerate((t, t_far)):
        base = other - z
        down2, up2 = base + z_at(-2), base + z_at(2)
        d_wait(down2)
        d_wait(up2)
        to = t - z
        go(d_send(9 + 3 * m, down2, to + z_at(1)))
        go(d_send(10 + 3 * m, down2, to + z_at(2)))
        go(d_send(11 + 3 * m, up2, to + z_at(-1)))

    w_wait(0, 3)
    go(w_on(3))

    @pl.when(y >= 2)
    def _():
        for i in range(4):
            w_own(i, 1).start()

    wait_q(2 * lo + 1 - c)
    wait_q(2 * (1 - lo) + 1 - c)

    def keep(n, b):
        return jnp.where(ids[4 * y + n] == b, 1.0, 0.0).astype(F32)

    for b in range(2):
        picked = qg4[0].astype(F32) * keep(0, b)
        for n in range(1, 4):
            picked = picked + qg4[n].astype(F32) * keep(n, b)
        qb[b] = picked.astype(BF16)
    for copy in locals_:
        copy.wait()

    @pl.when(y < 2)
    def _():
        for i in range(4):
            w_wait(1, i)

    @pl.when(y >= 2)
    def _():
        for i in range(4):
            w_wait(2, i)

    def chunk(d, k):
        return (z + 15 - k) % 8 if d == 0 else 8 + (z + 1 + k) % 8

    def hop(d, p, k):
        return remote(
            partial.at[chunk(d, k), p], ring.at[d, p, k],
            rs_sem.at[d, p, k], rr_sem.at[d, p, k], s, z_next if d == 0 else z_prev,
        )

    def store(p, value):
        partial[:, p] = value.reshape(NTP, 32, 2 * COLS).astype(BF16)
        for d in range(2):
            go(hop(d, p, 0))

    def advance(p, k):
        for d in range(2):
            hop(d, p, k - 1).wait_recv()
            partial[chunk(d, k), p] = (
                partial[chunk(d, k), p].astype(F32) + ring[d, p, k - 1].astype(F32)
            ).astype(BF16)
            if k < STEPS:
                go(hop(d, p, k))

    for p in range(4):
        picked = wg[0, 0 : 2 * COLS, :] * keep(p, 0).astype(BF16) + wg[
            1, 0 : 2 * COLS, :
        ] * keep(p, 1).astype(BF16)
        store(p, dot_nt(qg4[p], picked))

    def sum_low_rank():
        for peer in tp_peers:
            remote(bpart.at[peer], bland.at[peer], bs_sem.at[0], br_sem.at[peer], s, peer).wait_recv()
        bown[...] = jnp.sum(bland[...], axis=0).astype(BF16)
        for n, peer in enumerate(tp_peers):
            go(remote(bown, ball.at[t], cs_sem.at[n], cr_sem.at[t], s, peer))
        ball[t] = bown[...]

    def wait_hidden():
        for part in range(2):
            remote(
                hidden.at[:, window(lo, c, part)], hid4.at[2 * lo + 1 - c, part],
                hs_sem.at[0], hr_sem.at[part], sib, t,
            ).wait_recv()
            for i in range(2):
                for first, count, base in ((0, SPLIT, 2), (SPLIT, TOKENS - SPLIT, 6)):
                    remote(
                        hidden.at[pl.ds(first, count), window(lo, c, part)],
                        hid4.at[2 * (1 - lo) + i, part, pl.ds(first, count), :],
                        hs_sem.at[0], hr_sem.at[base + 2 * i + part], sib, t,
                    ).wait_recv()

    skip = pl.ds(pl.multiple_of(64 * c, 64), COLS)

    def weight_rows(yd):
        @pl.when(yd < 2)
        def _():
            for n in range(4):
                term = dot_tn(hid4[n, yd % 2], qg4[n])
                for b in range(2):
                    if n == 0:
                        acc[b] = term * keep(n, b)
                    else:
                        acc[b] += term * keep(n, b)

        @pl.when(yd >= 2)
        def _():
            for b in range(2):
                acc[b] = dot_tn(embw[yd % 2], qb[b])

    def x_copy(n):
        to_right = n in (0, 2, 3)
        return remote(dws.at[n], dwl.at[n], xs_sem.at[n], xr_sem.at[n], right if to_right else left, t)

    def weight_far():
        weight_rows(yo)
        for b in range(2):
            dws[b] = acc[b, skip, :].astype(BF16)
            go(x_copy(b))

    def weight_near(side):
        weight_rows((yr, yl)[side])
        base = 2 + 2 * side
        dws[base + 1 - side] = acc[1 - side, skip, :].astype(BF16)
        go(x_copy(base + 1 - side))
        x_copy(side).wait_recv()
        dws[base + side] = (acc[side, skip, :] + dwl[side].astype(F32)).astype(BF16)
        go(x_copy(base + side))

    def weight_own():
        weight_rows(y)

    def embed_part():
        @pl.when(y < 2)
        def _():
            for i in range(4):
                w_wait(2, i)

        @pl.when(y >= 2)
        def _():
            for i in range(4):
                w_wait(1, i)

        store(4, dot_nt(qb[0], wg[0, 2 * COLS :, :]) + dot_nt(qb[1], wg[1, 2 * COLS :, :]))

    def n_copy():
        return remote(nsend, nland, ns_sem.at[0], ns_sem.at[1], (s + NSEC - 1) % NSEC, t)

    def adapter_term():
        for i in range(1, 8):
            d_wait(hi * 8 + z_at(i)) if i not in (2, 6) else None
            d_wait((1 - hi) * 8 + z_at(i)) if i not in (2, 6) else None
        own = bown[:, 0:RANK]
        residual = res_ref[...].astype(F32)
        for n in range(NTP):
            term = dot_nt(own, dfull[n])
            if n < 8:
                nsend[n] = (residual[:, n * COLS : (n + 1) * COLS] + term).astype(BF16)
            else:
                for h in range(2):
                    apsend[2 * (n - 8) + h] = term[:, h * HD : (h + 1) * HD]
        go(n_copy())
        for n, peer in enumerate(section_peers):
            go(remote(apsend.at[peer], apland.at[s], as_sem.at[n], ar_sem.at[s], peer, t))
        apland[s] = apsend[s]

    for k in range(1, STEPS):
        for p in range(4):
            advance(p, k)
        if k == 1:
            sum_low_rank()
        if k == 2:
            wait_hidden()
            weight_far()
        if k == 3:
            embed_part()
            weight_near(0)
        if k == 4:
            advance(4, 1)
            weight_near(1)
        if k == 5:
            advance(4, 2)
            weight_own()
        if k == 6:
            advance(4, 3)
            adapter_term()

    def swap(p):
        return remote(
            partial.at[(1 - hi) * 8 + z, p], hland.at[p], is_sem.at[p], ir_sem.at[p], s, t_far
        )

    def move(src, dst, send_sem, recv_sem, here_sem, dest):
        away = remote(src, dst, send_sem, recv_sem, dest, t)
        near = pltpu.make_async_copy(src, dst, here_sem)

        @pl.when(dest != s)
        def _():
            away.start()

        @pl.when(dest == s)
        def _():
            near.start()

        def finish():
            @pl.when(dest != s)
            def _():
                away.wait_send()

            @pl.when(dest == s)
            def _():
                near.wait()

        return finish

    ends = []

    def joined_halves(p):
        swap(p).wait_recv()
        return partial[hi * 8 + z, p].astype(F32) + hland[p].astype(F32)

    for p in range(4):
        advance(p, STEPS)
        go(swap(p))
    advance(4, 4)
    for peer in tp_peers:
        remote(bown, ball.at[peer], cs_sem.at[0], cr_sem.at[peer], s, peer).wait_recv()
    ugt_ref[...] = dot_nn(qgt[...], ball[:, :, RANK : 2 * RANK].reshape(TOKENS, RANK))
    advance(4, 5)
    for p in range(4):
        total[p] = joined_halves(p).astype(BF16)
        dest = (y * 4 + p + NSEC - 1) % NSEC
        ends.append(move(total.at[p], pland.at[j], ps_sem.at[p], pr_sem.at[j], fin_sem.at[p], dest))
    advance(4, 6)
    fbuf[...] = dot_tn(jw[...], ball[:, :, 0:RANK].reshape(TOKENS, RANK))
    dg_ref[...] = fbuf[pl.ds(pl.multiple_of(64 * (z % 2), 64), COLS), :]
    for n in (2, 3, 4, 5):
        x_copy(n).wait_recv()
    for b in range(2):
        wsum_ref[b] = acc[b, skip, :] + (dwl[2 + b].astype(F32) + dwl[4 + b].astype(F32))
    advance(4, STEPS)
    go(swap(4))

    n_copy().wait_recv()
    for n in range(4):
        source = (((s + 1) % NSEC) // 4) * 4 + n

        @pl.when(source != s)
        def _():
            remote(total.at[n], pland.at[n], ps_sem.at[n], pr_sem.at[n], source, t).wait_recv()

    value = joined_halves(4)
    for n in range(4):
        etotal[n] = value[:, n * HD : (n + 1) * HD]
        dest = 2 * j + n % 2 + 8 * (n // 2)
        ends.append(
            move(etotal.at[n], eland.at[y], es_sem.at[n], er_sem.at[y], fin_sem.at[4 + n], dest)
        )
    for end in ends:
        end()
    more = jnp.where(s == NSEC - 1, 0.0, 1.0).astype(F32)
    for n in range(8):
        half = pland[n % 4].astype(F32)[:, (n // 4) * COLS : (n // 4 + 1) * COLS]
        passed_ref[:, n * COLS : (n + 1) * COLS] = (
            (nland[n].astype(F32) + half) * more
        ).astype(BF16)
    for peer in section_peers:
        remote(apsend.at[peer], apland.at[peer], as_sem.at[0], ar_sem.at[peer], peer, t).wait_recv()
    for n in range(4):
        source = n * 4 + (s % 8) // 2

        @pl.when(source != s)
        def _():
            remote(etotal.at[n], eland.at[n], es_sem.at[n], er_sem.at[n], source, t).wait_recv()

    embed_ref[...] = jnp.sum(eland[...], axis=0) + jnp.sum(apland[...], axis=0)
    for copy in sent:
        copy.wait_send()
    for i in range(4):
        w_own(i, 1).wait_send()


def whole_call(ids, q, k, v, g, seg, upt, down, residual, hidden, embedding, weight):
    vm = pl.BlockSpec(memory_space=pltpu.VMEM)
    sm = pl.BlockSpec(memory_space=pltpu.SMEM)
    anys = pl.BlockSpec(memory_space=pl.ANY)
    dma = pltpu.SemaphoreType.DMA
    out = jax.ShapeDtypeStruct
    return pl.pallas_call(
        whole_kernel,
        out_shape=(
            out((COLS, TOKENS), BF16),
            out((COLS, TOKENS), BF16),
            out((COLS, RANK), F32),
            out((COLS, RANK), F32),
            out((2, COLS, COLS), F32),
            out((32, WIDTH), BF16),
            out((32, HD), F32),
        ),
        in_specs=[sm] + [vm] * 8 + [anys] * 3,
        out_specs=(vm,) * 7,
        scratch_shapes=[
            pltpu.VMEM((TOKENS, COLS), BF16),
            pltpu.VMEM((COLS, TOKENS), BF16),
            pltpu.VMEM((4, TOKENS, COLS), BF16),
            pltpu.VMEM((4, 2, TOKENS, WIN), BF16),
            pltpu.VMEM((2, 4 * COLS, COLS), BF16),
            pltpu.VMEM((2, TOKENS, WIN), BF16),
            pltpu.VMEM((TOKENS, WIN), BF16),
            pltpu.VMEM((WIN, RANK), BF16),
            pltpu.VMEM((NTP, COLS, RANK), BF16),
            pltpu.VMEM((NTP, 32, 2 * RANK), F32),
            pltpu.VMEM((NTP, 32, 2 * RANK), F32),
            pltpu.VMEM((32, 2 * RANK), BF16),
            pltpu.VMEM((NTP, 32, 2 * RANK), BF16),
            pltpu.VMEM((NTP, PARTS, 32, 2 * COLS), BF16),
            pltpu.VMEM((2, PARTS, STEPS, 32, 2 * COLS), BF16),
            pltpu.VMEM((PARTS, 32, 2 * COLS), BF16),
            pltpu.VMEM((4, 32, 2 * COLS), BF16),
            pltpu.VMEM((4, 32, HD), F32),
            pltpu.VMEM((4, 32, 2 * COLS), BF16),
            pltpu.VMEM((4, 32, HD), F32),
            pltpu.VMEM((8, 32, COLS), BF16),
            pltpu.VMEM((8, 32, COLS), BF16),
            pltpu.VMEM((NSEC, 32, HD), F32),
            pltpu.VMEM((NSEC, 32, HD), F32),
            pltpu.VMEM((TOKENS, RANK), F32),
            pltpu.VMEM((2, TOKENS, COLS), BF16),
            pltpu.VMEM((2, WIN, COLS), F32),
            pltpu.VMEM((6, COLS, COLS), BF16),
            pltpu.VMEM((6, COLS, COLS), BF16),
            dma((9,)), dma((12,)), dma((12,)), dma((10,)), dma((10,)), dma((3,)), dma((4,)),
            dma((15,)), dma((16,)), dma((15,)), dma((16,)),
            dma((15,)), dma((16,)),
            dma((2, PARTS, STEPS)), dma((2, PARTS, STEPS)),
            dma((PARTS,)), dma((PARTS,)), dma((6,)), dma((6,)),
            dma((4,)), dma((4,)), dma((4,)), dma((4,)), dma((8,)), dma((2,)), dma((15,)), dma((16,)),
        ],
        compiler_params=pltpu.CompilerParams(
            collective_id=0, has_side_effects=True, vmem_limit_bytes=VMEM_LIMIT
        ),
        name="attention_block_backward",
    )(ids, q, k, v, g, seg, upt, down, residual, hidden, embedding, weight)


def copy_kernel(*refs):
    count = len(refs) // 2
    sems = refs[-1]
    copies = [
        pltpu.make_async_copy(refs[n], refs[count + n], sems.at[n]) for n in range(count)
    ]
    for copy in copies:
        copy.start()
    for copy in copies:
        copy.wait()


def copy_call(arrays):
    anys = pl.BlockSpec(memory_space=pl.ANY)
    return pl.pallas_call(
        copy_kernel,
        out_shape=tuple(jax.ShapeDtypeStruct(a.shape, a.dtype) for a in arrays),
        in_specs=[anys] * len(arrays),
        out_specs=(anys,) * len(arrays),
        scratch_shapes=[pltpu.SemaphoreType.DMA((len(arrays),))],
        compiler_params=pltpu.CompilerParams(vmem_limit_bytes=VMEM_LIMIT),
        name="hand_over",
    )(*arrays)


def on_device(
    saved_queries,
    saved_keys,
    values,
    attention_output_grad,
    segments,
    hidden,
    embedding,
    section_block_index,
    shared_query_weight,
    adapter_down_factor,
    adapter_up_factor,
    residual,
):
    results = whole_call(
        section_block_index[:, 0],
        saved_queries[0].T,
        saved_keys[0].T,
        values[0].T,
        attention_output_grad[0].T,
        segments[None, :],
        adapter_up_factor[0].T,
        adapter_down_factor[0],
        residual[0],
        hidden[0],
        embedding,
        shared_query_weight,
    )
    kgt, vgt, down_grad, ugt, weight_grad, passed, embed_grad = copy_call(results)
    return (
        kgt.T[None],
        vgt.T[None],
        down_grad[None],
        ugt.T[None],
        weight_grad,
        passed[None],
        embed_grad,
    )


def solution(mesh):
    in_specs = (
        P("section", None, "tp"),
        P("section", None, "tp"),
        P("section", None, "tp"),
        P("section", None, "tp"),
        P(),
        P("section", None, None),
        P(),
        P(),
        P(None, "section", "tp"),
        P("section", "tp", None),
        P("section", None, "tp"),
        P("section", "tp", None),
    )
    out_specs = (
        P("section", None, "tp"),
        P("section", None, "tp"),
        P("section", "tp", None),
        P("section", None, "tp"),
        P(None, "section", "tp"),
        P("section", "tp", None),
        P("tp", "section"),
    )
    return jax.shard_map(
        on_device, mesh=mesh, in_specs=in_specs, out_specs=out_specs, check_vma=False
    )
```

time: 142 us -> 238 us (1.68)
  the two profiles are of different devices: /device:TPU:25 before, /device:TPU:1 now
where the time goes in v3:
time: 238 us
  Pallas kernels  237 us (100%)
    pallas_call x1, Pallas kernels, whole_call(): pl.pallas_call(whole_kernel, out_shape=(out((COLS, TOKENS), BF16), out((C...  131 us
    pallas_call x1, Pallas kernels, copy_call(): pl.pallas_call(copy_kernel, out_shape=tuple((jax.ShapeDtypeStruct(a.shape...  106 us

profile of v3, /device:TPU:1, one launch (start us, length us, event | category | flops | bytes accessed | tf_op | source)
XLA Modules:
  0.0 238.0 jit_solution(7674994902626563783)
XLA Ops:
  0.6 130.8 %attention_block_backward.1 = (bf16[448,512]{1,0:T(8,128)(2,1)}, bf16[448,512]{1,0:T(8,128)(2,1)}, f32[448,128]{1,0:T(8,128)}, f32[448,128]{1,0:T(8,128)}, f32[2...) custom-call(s32[16]{0:T(128)} %bitcast.40, bf16[448,512]{1,0:T(8,128)(2,1)} %bitcast.32, ...), custom_call_target="tpu_custom_call" | custom-call | tf_op jit(solution)/shard_map/attention_block_backward/pallas_call | solution.py:532
  131.5 106.4 %hand_over.1 = (bf16[448,512]{1,0:T(8,128)(2,1)}, bf16[448,512]{1,0:T(8,128)(2,1)}, f32[448,128]{1,0:T(8,128)}, f32[448,128]{1,0:T(8,128)}, f32[2,448,448]{2,1,0...) custom-call(bf16[448,512]{1,0:T(8,128)(2,1)} %get-tuple-element.21.refs_0_, ...), custom_call_target="tpu_custom_call" | custom-call | tf_op jit(solution)/shard_map/hand_over/pallas_call | solution.py:603

commit v4 on v3

--- a/solution.py
+++ b/solution.py
@@ -14,9 +14,8 @@
 WIN = 512
 NSEC = 16
 NTP = 16
-SPLIT = 192
+SPLIT = 160
 STEPS = 7
-HALF = 224
 PARTS = 5
 VMEM_LIMIT = 60 * 1024 * 1024
 F32 = jnp.float32
@@ -79,13 +78,13 @@
 
 
 def whole_kernel(
-    ids, q_ref, k_ref, v_ref, g_ref, seg_ref, upt_ref, down_ref, res_ref, hidden, embedding, weight,
+    ids, q_hbm, k_hbm, v_hbm, g_hbm, seg_ref, upt_ref, down_ref, res_ref, hidden, embedding, weight,
     kg_ref, vg_ref, dg_ref, ugt_ref, wsum_ref, passed_ref, embed_ref,
-    qg, qgt, qg4, hid4, wg, embw, jw, adp, dfull, bpart, bland, bown, ball,
-    partial, ring, hland, total, etotal, pland, eland, nsend, nland, apsend, apland, fbuf, qb, acc, dws, dwl,
+    qg, qgt, qg4, hid4, wg, embw, jw, adp, adw, bgrp, bpart, bland, bown, ball,
+    heads, partial, ring, hland, total, etotal, pland, eland, nland, fbuf, qb, acc, dws, dwl,
     loc_sem, ws_sem, wr_sem, hs_sem, hr_sem, qs_sem, qr_sem, bs_sem, br_sem, cs_sem, cr_sem,
-    ds_sem, dr_sem, rs_sem, rr_sem, is_sem, ir_sem, xs_sem, xr_sem,
-    ps_sem, pr_sem, es_sem, er_sem, fin_sem, ns_sem, as_sem, ar_sem,
+    gs_sem, gr_sem, rs_sem, rr_sem, is_sem, ir_sem, xs_sem, xr_sem,
+    ps_sem, pr_sem, es_sem, er_sem, fin_sem, ns_sem,
 ):
     s = lax.axis_index("section")
     t = lax.axis_index("tp")
@@ -98,10 +97,15 @@
     t_far = (1 - hi) * 8 + z
     yl, yr, yo = (y + 3) % 4, (y + 1) % 4, (y + 2) % 4
     left, right = yl * 4 + j, yr * 4 + j
-    yin, yout = y + 1 - 2 * (y % 2), 3 - y
     z_next, z_prev = hi * 8 + (z + 1) % 8, hi * 8 + (z + 7) % 8
     tp_peers = [(t + i) % NTP for i in range(1, NTP)]
     section_peers = [(s + i) % NSEC for i in range(1, NSEC)]
+    loads = [
+        pltpu.make_async_copy(array, heads.at[n], loc_sem.at[9 + n])
+        for n, array in enumerate((q_hbm, k_hbm, v_hbm, g_hbm))
+    ]
+    for load in loads:
+        load.start()
     greet(
         [(p, t) for p in section_peers]
         + [(s, p) for p in tp_peers]
@@ -114,67 +118,62 @@
         sent.append(copy)
         return copy
 
-    def piece(i, owner_y):
-        first = pl.multiple_of(owner_y * COLS + HALF * (i % 2), 32)
-        return wg.at[i // 2, pl.ds(first, HALF), :]
-
-    def w_own(i, to_in):
-        n = 4 * to_in + i
+    def row_block(b, owner_y):
+        return wg.at[b, pl.ds(pl.multiple_of(owner_y * COLS, 64), COLS), :]
+
+    for n, (b, dest, slot) in enumerate([(0, right, 0), (1, left, 3), (1, right, 1), (0, left, 2)]):
+        go(remote(weight.at[b], row_block(b, y), ws_sem.at[n], wr_sem.at[slot], dest, t))
+
+    def w_on(n, b, owner_y, dest):
+        return remote(row_block(b, owner_y), row_block(b, owner_y), ws_sem.at[n], wr_sem.at[n], dest, t)
+
+    def w_wait(b, owner_y, slot):
+        remote(weight.at[b], row_block(b, owner_y), ws_sem.at[0], wr_sem.at[slot], left, t).wait_recv()
+
+    adder = t % 4
+    half = (t // 4) % 2
+    mine = pl.ds(pl.multiple_of(half * COLS, 64), COLS)
+    rest = pl.ds(pl.multiple_of((1 - half) * COLS, 64), COLS)
+
+    def down_copy(n):
+        return remote(down_ref, adw.at[n, mine, :], gs_sem.at[0], gr_sem.at[n], y * 4 + adder, t)
+
+    def back_copy(n):
         return remote(
-            weight.at[i // 2, pl.ds(HALF * (i % 2), HALF), :], piece(i, y),
-            ws_sem.at[n], wr_sem.at[n], (yin if to_in else yout) * 4 + j, t,
+            ball.at[:, :, pl.ds(0, RANK)], bgrp.at[n], gs_sem.at[1], gr_sem.at[4 + n], y * 4 + adder, t
         )
 
-    def w_on(i):
-        return remote(
-            piece(i, yout), piece(i, yout), ws_sem.at[8 + i], wr_sem.at[8 + i], yin * 4 + j, t
-        )
-
-    def w_wait(kind, i):
-        owner = (yout, yin, 3 - yin)[kind]
-        n = 4 * kind + i
-        remote(piece(i, owner), piece(i, owner), ws_sem.at[0], wr_sem.at[n], yin * 4 + j, t).wait_recv()
-
-    @pl.when(y < 2)
-    def _():
-        for i in range(4):
-            w_own(i, 1).start()
-
-    for i in range(4):
-        go(w_own(i, 0))
-
-    def z_at(step):
-        return (z + step + 8) % 8
-
-    def d_send(n, slot, to):
-        return remote(dfull.at[slot], dfull.at[slot], ds_sem.at[n], dr_sem.at[slot], s, to)
-
-    def d_wait(slot):
-        d_send(0, slot, t_far).wait_recv()
-
-    dfull[t] = down_ref[...]
-    for n, to in enumerate([t_far] + [hi * 8 + z_at(i) for i in (1, -1, 2, -2)]):
-        go(d_send(n, t, to))
+    adw[:, rest, :] = jnp.zeros((4, COLS, RANK), BF16)
+
+    @pl.when(j != adder)
+    def _():
+        down_copy(j).start()
+
+    @pl.when(j == adder)
+    def _():
+        adw[j, mine, :] = down_ref[...]
 
     def window(lo_d, c_d, part):
         return pl.ds(pl.multiple_of(896 * lo_d + 384 * c_d + 1792 * part, 128), WIN)
 
-    def send_hidden(part):
-        n = 5 * part
+    def send_far(part):
+        for i in range(2):
+            go(remote(
+                hidden.at[pl.ds(SPLIT, TOKENS - SPLIT), window(1 - lo, i, part)],
+                hid4.at[j, part, pl.ds(SPLIT, TOKENS - SPLIT), :],
+                hs_sem.at[5 * part + i], hr_sem.at[6 + 2 * c + part], across[i], t_far,
+            ))
+
+    def send_near(part):
         for i in range(2):
             go(remote(
                 hidden.at[pl.ds(0, SPLIT), window(1 - lo, i, part)],
                 hid4.at[j, part, pl.ds(0, SPLIT), :],
-                hs_sem.at[n + 2 * i], hr_sem.at[2 + 2 * c + part], across[i], t,
-            ))
-            go(remote(
-                hidden.at[pl.ds(SPLIT, TOKENS - SPLIT), window(1 - lo, i, part)],
-                hid4.at[j, part, pl.ds(SPLIT, TOKENS - SPLIT), :],
-                hs_sem.at[n + 2 * i + 1], hr_sem.at[6 + 2 * c + part], across[i], t_far,
+                hs_sem.at[5 * part + 2 + i], hr_sem.at[2 + 2 * c + part], across[i], t,
             ))
         go(remote(
             hidden.at[:, window(lo, 1 - c, part)], hid4.at[j, part],
-            hs_sem.at[n + 4], hr_sem.at[part], sib, t,
+            hs_sem.at[5 * part + 4], hr_sem.at[part], sib, t,
         ))
 
     locals_ = []
@@ -196,68 +195,70 @@
     def _():
         from_embedding.start()
 
-    send_hidden(0)
+    send_far(0)
     for b in range(2):
-        here(weight.at[b], wg.at[b, pl.ds(pl.multiple_of(y * COLS, 64), COLS), :])
+        here(weight.at[b], row_block(b, y))
     for part in range(2):
         here(hidden.at[:, window(lo, c, part)], hid4.at[j, part])
         here(embedding.at[:, window(lo, c, part)], embw.at[part])
 
-    attention(q_ref, k_ref, v_ref, g_ref, seg_ref, qg, qgt, kg_ref, vg_ref)
+    n_copy = remote(res_ref, nland, ns_sem.at[0], ns_sem.at[1], (s + NSEC - 1) % NSEC, t)
+
+    for load in loads:
+        load.wait()
+    attention(
+        heads.at[0], heads.at[1], heads.at[2], heads.at[3], seg_ref, qg, qgt, kg_ref, vg_ref
+    )
 
     go(remote(qg, qg4.at[j], qs_sem.at[0], qr_sem.at[j], partner, t))
     go(remote(qg, qg4.at[j], qs_sem.at[1], qr_sem.at[j], sib, t))
     qg4[j] = qg[...]
 
-    w_wait(0, 0)
-    go(w_on(0))
-
-    d_wait(t_far)
-    for n, to in enumerate([hi * 8 + z_at(i) for i in (1, -1, 2, -2)]):
-        go(d_send(5 + n, t_far, to))
-
     adp[...] = jnp.zeros_like(adp)
     adp[pl.ds(pl.multiple_of(64 * (z % 2), 64), COLS), :] = down_ref[...]
-    bpart[:, :, 0:RANK] = dot_nn(qg[...], upt_ref[...]).reshape(NTP, 32, RANK)
+    bpart[:, :, 0:RANK] = dot_nn(qg[...], upt_ref[...]).reshape(NTP, 32, RANK).astype(BF16)
     from_hidden.wait()
-    bpart[:, :, RANK : 2 * RANK] = dot_nn(jw[...], adp[...]).reshape(NTP, 32, RANK)
+    bpart[:, :, RANK : 2 * RANK] = dot_nn(jw[...], adp[...]).reshape(NTP, 32, RANK).astype(BF16)
     for n, peer in enumerate(tp_peers):
         go(remote(bpart.at[peer], bland.at[t], bs_sem.at[n], br_sem.at[t], s, peer))
     bland[t] = bpart[t]
-
-    w_wait(0, 1)
-    go(w_on(1))
-    send_hidden(1)
+    send_near(0)
+
+    w_wait(0, yl, 0)
+    go(w_on(4, 0, yl, right))
+    w_wait(1, yr, 3)
+    go(w_on(5, 1, yr, left))
+
+    for peer in tp_peers:
+        remote(bpart.at[peer], bland.at[peer], bs_sem.at[0], br_sem.at[peer], s, peer).wait_recv()
+    bown[...] = jnp.sum(bland[...].astype(F32), axis=0).astype(BF16)
+    for n, peer in enumerate(tp_peers):
+        go(remote(bown, ball.at[t], cs_sem.at[n], cr_sem.at[t], s, peer))
+    ball[t] = bown[...]
 
     def wait_q(slot):
         remote(qg, qg4.at[slot], qs_sem.at[0], qr_sem.at[slot], sib, t).wait_recv()
 
-    w_wait(0, 2)
-    go(w_on(2))
     slot_partner = 2 * (1 - lo) + c
     wait_q(slot_partner)
     go(remote(
         qg4.at[slot_partner], qg4.at[slot_partner], qs_sem.at[2], qr_sem.at[slot_partner], sib, t
     ))
 
-    for m, other in enumerate((t, t_far)):
-        base = other - z
-        down2, up2 = base + z_at(-2), base + z_at(2)
-        d_wait(down2)
-        d_wait(up2)
-        to = t - z
-        go(d_send(9 + 3 * m, down2, to + z_at(1)))
-        go(d_send(10 + 3 * m, down2, to + z_at(2)))
-        go(d_send(11 + 3 * m, up2, to + z_at(-1)))
-
-    w_wait(0, 3)
-    go(w_on(3))
-
-    @pl.when(y >= 2)
-    def _():
-        for i in range(4):
-            w_own(i, 1).start()
-
+    for peer in tp_peers:
+        remote(bown, ball.at[peer], cs_sem.at[0], cr_sem.at[peer], s, peer).wait_recv()
+
+    @pl.when(j != adder)
+    def _():
+        back_copy(j).start()
+
+    @pl.when(j == adder)
+    def _():
+        bgrp[j] = ball[:, :, 0:RANK]
+
+    send_far(1)
+    send_near(1)
+    go(n_copy)
     wait_q(2 * lo + 1 - c)
     wait_q(2 * (1 - lo) + 1 - c)
 
@@ -272,15 +273,18 @@
     for copy in locals_:
         copy.wait()
 
-    @pl.when(y < 2)
-    def _():
-        for i in range(4):
-            w_wait(1, i)
-
-    @pl.when(y >= 2)
-    def _():
-        for i in range(4):
-            w_wait(2, i)
+    @pl.when(j == adder)
+    def _():
+        for n in range(4):
+            @pl.when(j != n)
+            def _():
+                down_copy(n).wait_recv()
+                back_copy(n).wait_recv()
+
+    w_wait(1, yl, 1)
+    w_wait(0, yr, 2)
+    w_wait(0, yo, 4)
+    w_wait(1, yo, 5)
 
     def chunk(d, k):
         return (z + 15 - k) % 8 if d == 0 else 8 + (z + 1 + k) % 8
@@ -291,8 +295,8 @@
             rs_sem.at[d, p, k], rr_sem.at[d, p, k], s, z_next if d == 0 else z_prev,
         )
 
-    def store(p, value):
-        partial[:, p] = value.reshape(NTP, 32, 2 * COLS).astype(BF16)
+    def store(p):
+        partial[:, p] = fbuf[...].reshape(NTP, 32, 2 * COLS).astype(BF16)
         for d in range(2):
             go(hop(d, p, 0))
 
@@ -309,15 +313,21 @@
         picked = wg[0, 0 : 2 * COLS, :] * keep(p, 0).astype(BF16) + wg[
             1, 0 : 2 * COLS, :
         ] * keep(p, 1).astype(BF16)
-        store(p, dot_nt(qg4[p], picked))
-
-    def sum_low_rank():
-        for peer in tp_peers:
-            remote(bpart.at[peer], bland.at[peer], bs_sem.at[0], br_sem.at[peer], s, peer).wait_recv()
-        bown[...] = jnp.sum(bland[...], axis=0).astype(BF16)
-        for n, peer in enumerate(tp_peers):
-            go(remote(bown, ball.at[t], cs_sem.at[n], cr_sem.at[t], s, peer))
-        ball[t] = bown[...]
+        fbuf[...] = dot_nt(qg4[p], picked)
+
+        @pl.when((j == adder) & (t < 8))
+        def _():
+            fbuf[...] += dot_nt(bgrp[p].reshape(TOKENS, RANK), adw[p])
+
+        store(p)
+    fbuf[...] = dot_nt(qb[0], wg[0, 2 * COLS :, :]) + dot_nt(qb[1], wg[1, 2 * COLS :, :])
+
+    @pl.when((j == adder) & (t >= 8))
+    def _():
+        for n in range(4):
+            fbuf[...] += dot_nt(bgrp[n].reshape(TOKENS, RANK), adw[n])
+
+    store(4)
 
     def wait_hidden():
         for part in range(2):
@@ -364,69 +374,37 @@
     def weight_near(side):
         weight_rows((yr, yl)[side])
         base = 2 + 2 * side
-        dws[base + 1 - side] = acc[1 - side, skip, :].astype(BF16)
+        for b in (1 - side, side):
+            dws[base + b] = acc[b, skip, :].astype(BF16)
         go(x_copy(base + 1 - side))
+
+    def weight_on(side):
         x_copy(side).wait_recv()
-        dws[base + side] = (acc[side, skip, :] + dwl[side].astype(F32)).astype(BF16)
-        go(x_copy(base + side))
+        n = 2 + 3 * side
+        dws[n] = (dws[n].astype(F32) + dwl[side].astype(F32)).astype(BF16)
+        go(x_copy(n))
 
     def weight_own():
         weight_rows(y)
 
-    def embed_part():
-        @pl.when(y < 2)
-        def _():
-            for i in range(4):
-                w_wait(2, i)
-
-        @pl.when(y >= 2)
-        def _():
-            for i in range(4):
-                w_wait(1, i)
-
-        store(4, dot_nt(qb[0], wg[0, 2 * COLS :, :]) + dot_nt(qb[1], wg[1, 2 * COLS :, :]))
-
-    def n_copy():
-        return remote(nsend, nland, ns_sem.at[0], ns_sem.at[1], (s + NSEC - 1) % NSEC, t)
-
-    def adapter_term():
-        for i in range(1, 8):
-            d_wait(hi * 8 + z_at(i)) if i not in (2, 6) else None
-            d_wait((1 - hi) * 8 + z_at(i)) if i not in (2, 6) else None
-        own = bown[:, 0:RANK]
-        residual = res_ref[...].astype(F32)
-        for n in range(NTP):
-            term = dot_nt(own, dfull[n])
-            if n < 8:
-                nsend[n] = (residual[:, n * COLS : (n + 1) * COLS] + term).astype(BF16)
-            else:
-                for h in range(2):
-                    apsend[2 * (n - 8) + h] = term[:, h * HD : (h + 1) * HD]
-        go(n_copy())
-        for n, peer in enumerate(section_peers):
-            go(remote(apsend.at[peer], apland.at[s], as_sem.at[n], ar_sem.at[s], peer, t))
-        apland[s] = apsend[s]
-
     for k in range(1, STEPS):
-        for p in range(4):
+        for p in range(PARTS):
             advance(p, k)
         if k == 1:
-            sum_low_rank()
+            ugt_ref[...] = dot_nn(qgt[...], ball[:, :, RANK : 2 * RANK].reshape(TOKENS, RANK))
+            fbuf[:, 0:RANK] = dot_tn(jw[...], ball[:, :, 0:RANK].reshape(TOKENS, RANK))
+            dg_ref[...] = fbuf[pl.ds(pl.multiple_of(64 * (z % 2), 64), COLS), 0:RANK]
         if k == 2:
             wait_hidden()
             weight_far()
         if k == 3:
-            embed_part()
             weight_near(0)
+            weight_near(1)
         if k == 4:
-            advance(4, 1)
-            weight_near(1)
+            weight_on(0)
+            weight_on(1)
         if k == 5:
-            advance(4, 2)
             weight_own()
-        if k == 6:
-            advance(4, 3)
-            adapter_term()
 
     def swap(p):
         return remote(
@@ -462,36 +440,17 @@
         swap(p).wait_recv()
         return partial[hi * 8 + z, p].astype(F32) + hland[p].astype(F32)
 
-    for p in range(4):
+    for p in range(PARTS):
         advance(p, STEPS)
         go(swap(p))
-    advance(4, 4)
-    for peer in tp_peers:
-        remote(bown, ball.at[peer], cs_sem.at[0], cr_sem.at[peer], s, peer).wait_recv()
-    ugt_ref[...] = dot_nn(qgt[...], ball[:, :, RANK : 2 * RANK].reshape(TOKENS, RANK))
-    advance(4, 5)
+    for n in (2, 3, 4, 5):
+        x_copy(n).wait_recv()
+    for b in range(2):
+        wsum_ref[b] = acc[b, skip, :] + (dwl[2 + b].astype(F32) + dwl[4 + b].astype(F32))
     for p in range(4):
         total[p] = joined_halves(p).astype(BF16)
         dest = (y * 4 + p + NSEC - 1) % NSEC
         ends.append(move(total.at[p], pland.at[j], ps_sem.at[p], pr_sem.at[j], fin_sem.at[p], dest))
-    advance(4, 6)
-    fbuf[...] = dot_tn(jw[...], ball[:, :, 0:RANK].reshape(TOKENS, RANK))
-    dg_ref[...] = fbuf[pl.ds(pl.multiple_of(64 * (z % 2), 64), COLS), :]
-    for n in (2, 3, 4, 5):
-        x_copy(n).wait_recv()
-    for b in range(2):
-        wsum_ref[b] = acc[b, skip, :] + (dwl[2 + b].astype(F32) + dwl[4 + b].astype(F32))
-    advance(4, STEPS)
-    go(swap(4))
-
-    n_copy().wait_recv()
-    for n in range(4):
-        source = (((s + 1) % NSEC) // 4) * 4 + n
-
-        @pl.when(source != s)
-        def _():
-            remote(total.at[n], pland.at[n], ps_sem.at[n], pr_sem.at[n], source, t).wait_recv()
-
     value = joined_halves(4)
     for n in range(4):
         etotal[n] = value[:, n * HD : (n + 1) * HD]
@@ -499,16 +458,22 @@
         ends.append(
             move(etotal.at[n], eland.at[y], es_sem.at[n], er_sem.at[y], fin_sem.at[4 + n], dest)
         )
+    n_copy.wait_recv()
+    for n in range(4):
+        source = (((s + 1) % NSEC) // 4) * 4 + n
+
+        @pl.when(source != s)
+        def _():
+            remote(total.at[n], pland.at[n], ps_sem.at[n], pr_sem.at[n], source, t).wait_recv()
+
     for end in ends:
         end()
     more = jnp.where(s == NSEC - 1, 0.0, 1.0).astype(F32)
     for n in range(8):
         half = pland[n % 4].astype(F32)[:, (n // 4) * COLS : (n // 4 + 1) * COLS]
         passed_ref[:, n * COLS : (n + 1) * COLS] = (
-            (nland[n].astype(F32) + half) * more
+            (nland[:, n * COLS : (n + 1) * COLS].astype(F32) + half) * more
         ).astype(BF16)
-    for peer in section_peers:
-        remote(apsend.at[peer], apland.at[peer], as_sem.at[0], ar_sem.at[peer], peer, t).wait_recv()
     for n in range(4):
         source = n * 4 + (s % 8) // 2
 
@@ -516,11 +481,14 @@
         def _():
             remote(etotal.at[n], eland.at[n], es_sem.at[n], er_sem.at[n], source, t).wait_recv()
 
-    embed_ref[...] = jnp.sum(eland[...], axis=0) + jnp.sum(apland[...], axis=0)
+    embed_ref[...] = jnp.sum(eland[...], axis=0)
     for copy in sent:
         copy.wait_send()
-    for i in range(4):
-        w_own(i, 1).wait_send()
+
+    @pl.when(j != adder)
+    def _():
+        down_copy(j).wait_send()
+        back_copy(j).wait_send()
 
 
 def whole_call(ids, q, k, v, g, seg, upt, down, residual, hidden, embedding, weight):
@@ -540,7 +508,7 @@
             out((32, WIDTH), BF16),
             out((32, HD), F32),
         ),
-        in_specs=[sm] + [vm] * 8 + [anys] * 3,
+        in_specs=[sm] + [anys] * 4 + [vm] * 3 + [anys] * 4,
         out_specs=(vm,) * 7,
         scratch_shapes=[
             pltpu.VMEM((TOKENS, COLS), BF16),
@@ -551,11 +519,13 @@
             pltpu.VMEM((2, TOKENS, WIN), BF16),
             pltpu.VMEM((TOKENS, WIN), BF16),
             pltpu.VMEM((WIN, RANK), BF16),
-            pltpu.VMEM((NTP, COLS, RANK), BF16),
-            pltpu.VMEM((NTP, 32, 2 * RANK), F32),
-            pltpu.VMEM((NTP, 32, 2 * RANK), F32),
+            pltpu.VMEM((4, 2 * COLS, RANK), BF16),
+            pltpu.VMEM((4, NTP, 32, RANK), BF16),
+            pltpu.VMEM((NTP, 32, 2 * RANK), BF16),
+            pltpu.VMEM((NTP, 32, 2 * RANK), BF16),
             pltpu.VMEM((32, 2 * RANK), BF16),
             pltpu.VMEM((NTP, 32, 2 * RANK), BF16),
+            pltpu.VMEM((4, COLS, TOKENS), BF16),
             pltpu.VMEM((NTP, PARTS, 32, 2 * COLS), BF16),
             pltpu.VMEM((2, PARTS, STEPS, 32, 2 * COLS), BF16),
             pltpu.VMEM((PARTS, 32, 2 * COLS), BF16),
@@ -563,21 +533,18 @@
             pltpu.VMEM((4, 32, HD), F32),
             pltpu.VMEM((4, 32, 2 * COLS), BF16),
             pltpu.VMEM((4, 32, HD), F32),
-            pltpu.VMEM((8, 32, COLS), BF16),
-            pltpu.VMEM((8, 32, COLS), BF16),
-            pltpu.VMEM((NSEC, 32, HD), F32),
-            pltpu.VMEM((NSEC, 32, HD), F32),
-            pltpu.VMEM((TOKENS, RANK), F32),
+            pltpu.VMEM((32, WIDTH), BF16),
+            pltpu.VMEM((TOKENS, 2 * COLS), F32),
             pltpu.VMEM((2, TOKENS, COLS), BF16),
             pltpu.VMEM((2, WIN, COLS), F32),
             pltpu.VMEM((6, COLS, COLS), BF16),
             pltpu.VMEM((6, COLS, COLS), BF16),
-            dma((9,)), dma((12,)), dma((12,)), dma((10,)), dma((10,)), dma((3,)), dma((4,)),
+            dma((13,)), dma((6,)), dma((6,)), dma((10,)), dma((10,)), dma((3,)), dma((4,)),
             dma((15,)), dma((16,)), dma((15,)), dma((16,)),
-            dma((15,)), dma((16,)),
+            dma((2,)), dma((8,)),
             dma((2, PARTS, STEPS)), dma((2, PARTS, STEPS)),
             dma((PARTS,)), dma((PARTS,)), dma((6,)), dma((6,)),
-            dma((4,)), dma((4,)), dma((4,)), dma((4,)), dma((8,)), dma((2,)), dma((15,)), dma((16,)),
+            dma((4,)), dma((4,)), dma((4,)), dma((4,)), dma((8,)), dma((2,)),
         ],
         compiler_params=pltpu.CompilerParams(
             collective_id=0, has_side_effects=True, vmem_limit_bytes=VMEM_LIMIT
@@ -587,14 +554,17 @@
 
 
 def copy_kernel(*refs):
-    count = len(refs) // 2
+    count = (len(refs) - 1) // 3
     sems = refs[-1]
-    copies = [
-        pltpu.make_async_copy(refs[n], refs[count + n], sems.at[n]) for n in range(count)
-    ]
-    for copy in copies:
+    ins, outs, held = refs[:count], refs[count : 2 * count], refs[2 * count : 3 * count]
+    coming = [pltpu.make_async_copy(ins[n], held[n], sems.at[0, n]) for n in range(count)]
+    going = [pltpu.make_async_copy(held[n], outs[n], sems.at[1, n]) for n in range(count)]
+    for copy in coming:
         copy.start()
-    for copy in copies:
+    for n in range(count):
+        coming[n].wait()
+        going[n].start()
+    for copy in going:
         copy.wait()
 
 
@@ -605,7 +575,8 @@
         out_shape=tuple(jax.ShapeDtypeStruct(a.shape, a.dtype) for a in arrays),
         in_specs=[anys] * len(arrays),
         out_specs=(anys,) * len(arrays),
-        scratch_shapes=[pltpu.SemaphoreType.DMA((len(arrays),))],
+        scratch_shapes=[pltpu.VMEM(a.shape, a.dtype) for a in arrays]
+        + [pltpu.SemaphoreType.DMA((2, len(arrays)))],
         compiler_params=pltpu.CompilerParams(vmem_limit_bytes=VMEM_LIMIT),
         name="hand_over",
     )(*arrays)

time: 238 us -> 109 us (0.46)
  Pallas kernels: 237 us -> 109 us
    pallas_call x1, Pallas kernels: 106 us -> 3.35 us  [copy_call(): pl.pallas_call(copy_kernel, out_shape=tuple((jax.ShapeDtypeStruct(a.shape...]
    pallas_call x1, Pallas kernels: 131 us -> 105 us  [whole_call(): pl.pallas_call(whole_kernel, out_shape=(out((COLS, TOKENS), BF16), out((C...]
where the time goes in v4:
time: 109 us
  Pallas kernels  109 us (100%)
    pallas_call x1, Pallas kernels, whole_call(): pl.pallas_call(whole_kernel, out_shape=(out((COLS, TOKENS), BF16), out((C...  105 us
    pallas_call x1, Pallas kernels, copy_call(): pl.pallas_call(copy_kernel, out_shape=tuple((jax.ShapeDtypeStruct(a.shape...  3.35 us

profile of v4, /device:TPU:1, one launch (start us, length us, event | category | flops | bytes accessed | tf_op | source)
XLA Modules:
  0.0 109.4 jit_solution(14270076261363812777)
XLA Ops:
  0.6 105.2 %attention_block_backward.1 = (bf16[448,512]{1,0:T(8,128)(2,1)}, bf16[448,512]{1,0:T(8,128)(2,1)}, f32[448,128]{1,0:T(8,128)}, f32[448,128]{1,0:T(8,128)}, f32[2...) custom-call(s32[16]{0:T(128)} %bitcast.40, bf16[448,512]{1,0:T(8,128)(2,1)} %bitcast.32, ...), custom_call_target="tpu_custom_call" | custom-call | tf_op jit(solution)/shard_map/attention_block_backward/pallas_call | solution.py:500
  105.8 3.4 %hand_over.1 = (bf16[448,512]{1,0:T(8,128)(2,1)}, bf16[448,512]{1,0:T(8,128)(2,1)}, f32[448,128]{1,0:T(8,128)}, f32[448,128]{1,0:T(8,128)}, f32[2,448,448]{2,1,0...) custom-call(bf16[448,512]{1,0:T(8,128)(2,1)} %get-tuple-element.21.refs_0_, ...), custom_call_target="tpu_custom_call" | custom-call | tf_op jit(solution)/shard_map/hand_over/pallas_call | solution.py:573

commit v5 on v4

--- a/solution.py
+++ b/solution.py
@@ -16,7 +16,7 @@
 NTP = 16
 SPLIT = 160
 STEPS = 7
-PARTS = 5
+PARTS = 4
 VMEM_LIMIT = 60 * 1024 * 1024
 F32 = jnp.float32
 BF16 = jnp.bfloat16
@@ -81,10 +81,10 @@
     ids, q_hbm, k_hbm, v_hbm, g_hbm, seg_ref, upt_ref, down_ref, res_ref, hidden, embedding, weight,
     kg_ref, vg_ref, dg_ref, ugt_ref, wsum_ref, passed_ref, embed_ref,
     qg, qgt, qg4, hid4, wg, embw, jw, adp, adw, bgrp, bpart, bland, bown, ball,
-    heads, partial, ring, hland, total, etotal, pland, eland, nland, fbuf, qb, acc, dws, dwl,
+    heads, partial, ring, pland, nland, ebuf, eyl, epart, ering, efin, fbuf, qb, acc, dws, dwl,
     loc_sem, ws_sem, wr_sem, hs_sem, hr_sem, qs_sem, qr_sem, bs_sem, br_sem, cs_sem, cr_sem,
-    gs_sem, gr_sem, rs_sem, rr_sem, is_sem, ir_sem, xs_sem, xr_sem,
-    ps_sem, pr_sem, es_sem, er_sem, fin_sem, ns_sem,
+    gs_sem, gr_sem, rs_sem, rr_sem, xs_sem, xr_sem,
+    ps_sem, pr_sem, es_sem, er_sem, fin_sem, ns_sem, ys_sem, yr_sem, us_sem, ur_sem,
 ):
     s = lax.axis_index("section")
     t = lax.axis_index("tp")
@@ -109,7 +109,7 @@
     greet(
         [(p, t) for p in section_peers]
         + [(s, p) for p in tp_peers]
-        + [(a, t_far) for a in across]
+        + [(p, t_far) for p in section_peers]
     )
     sent = []
 
@@ -309,6 +309,51 @@
             if k < STEPS:
                 go(hop(d, p, k))
 
+    for n in range(4):
+        cols = pl.ds(2 * COLS + n * HD, HD)
+        fbuf[:, 0:HD] = dot_nt(qb[0], wg[0, cols, :]) + dot_nt(qb[1], wg[1, cols, :])
+
+        @pl.when((j == adder) & (t >= 8))
+        def _():
+            for m in range(4):
+                fbuf[:, 0:HD] += dot_nt(
+                    bgrp[m].reshape(TOKENS, RANK), adw[m, n * HD : (n + 1) * HD, :]
+                )
+
+        ebuf[n] = fbuf[:, 0:HD].astype(BF16)
+
+    def e_copy(i):
+        yd = (y + i) % 4
+        return remote(ebuf.at[yd], eyl.at[y], ys_sem.at[i - 1], yr_sem.at[y], yd * 4 + j, t)
+
+    for i in (1, 3, 2):
+        go(e_copy(i))
+
+    def e_hop(d, k):
+        return remote(
+            epart.at[chunk(d, k)], ering.at[d, k], us_sem.at[d, k], ur_sem.at[d, k],
+            s, z_next if d == 0 else z_prev,
+        )
+
+    def e_start():
+        value = ebuf[y].astype(F32)
+        for i in (1, 3, 2):
+            ys = (y + i) % 4
+            remote(ebuf.at[ys], eyl.at[ys], ys_sem.at[0], yr_sem.at[ys], s, t).wait_recv()
+            value = value + eyl[ys].astype(F32)
+        epart[...] = value.reshape(NTP, 32, HD).astype(BF16)
+        for d in range(2):
+            go(e_hop(d, 0))
+
+    def e_advance(k):
+        for d in range(2):
+            e_hop(d, k - 1).wait_recv()
+            epart[chunk(d, k)] = (
+                epart[chunk(d, k)].astype(F32) + ering[d, k - 1].astype(F32)
+            ).astype(BF16)
+            if k < STEPS:
+                go(e_hop(d, k))
+
     for p in range(4):
         picked = wg[0, 0 : 2 * COLS, :] * keep(p, 0).astype(BF16) + wg[
             1, 0 : 2 * COLS, :
@@ -320,14 +365,6 @@
             fbuf[...] += dot_nt(bgrp[p].reshape(TOKENS, RANK), adw[p])
 
         store(p)
-    fbuf[...] = dot_nt(qb[0], wg[0, 2 * COLS :, :]) + dot_nt(qb[1], wg[1, 2 * COLS :, :])
-
-    @pl.when((j == adder) & (t >= 8))
-    def _():
-        for n in range(4):
-            fbuf[...] += dot_nt(bgrp[n].reshape(TOKENS, RANK), adw[n])
-
-    store(4)
 
     def wait_hidden():
         for part in range(2):
@@ -365,17 +402,28 @@
         to_right = n in (0, 2, 3)
         return remote(dws.at[n], dwl.at[n], xs_sem.at[n], xr_sem.at[n], right if to_right else left, t)
 
+    upper = pl.ds(pl.multiple_of(64 * c, 32), HD)
+    lower = pl.ds(pl.multiple_of(64 * c + HD, 32), HD)
+
+    def stack(n, b):
+        for i in range(3):
+            dws[n, i * COLS : (i + 1) * COLS, :] = acc[
+                b, skip, i * RANK : (i + 1) * RANK
+            ].astype(BF16)
+        ends_ = jnp.concatenate([acc[b, upper, 3 * RANK : COLS], acc[b, lower, 3 * RANK : COLS]], axis=1)
+        dws[n, 3 * COLS : 3 * COLS + HD, :] = ends_.astype(BF16)
+
     def weight_far():
         weight_rows(yo)
         for b in range(2):
-            dws[b] = acc[b, skip, :].astype(BF16)
+            stack(b, b)
             go(x_copy(b))
 
     def weight_near(side):
         weight_rows((yr, yl)[side])
         base = 2 + 2 * side
         for b in (1 - side, side):
-            dws[base + b] = acc[b, skip, :].astype(BF16)
+            stack(base + b, b)
         go(x_copy(base + 1 - side))
 
     def weight_on(side):
@@ -390,6 +438,10 @@
     for k in range(1, STEPS):
         for p in range(PARTS):
             advance(p, k)
+            if p == 1 and k == 2:
+                e_start()
+            if p == 1 and k > 2:
+                e_advance(k - 2)
         if k == 1:
             ugt_ref[...] = dot_nn(qgt[...], ball[:, :, RANK : 2 * RANK].reshape(TOKENS, RANK))
             fbuf[:, 0:RANK] = dot_tn(jw[...], ball[:, :, 0:RANK].reshape(TOKENS, RANK))
@@ -405,83 +457,91 @@
             weight_on(1)
         if k == 5:
             weight_own()
-
-    def swap(p):
-        return remote(
-            partial.at[(1 - hi) * 8 + z, p], hland.at[p], is_sem.at[p], ir_sem.at[p], s, t_far
-        )
-
-    def move(src, dst, send_sem, recv_sem, here_sem, dest):
-        away = remote(src, dst, send_sem, recv_sem, dest, t)
+        if k == 6:
+            e_advance(5)
+
+    ends = []
+
+    def move(src, dst, send_sem, recv_sem, here_sem, section, tp):
+        away = remote(src, dst, send_sem, recv_sem, section, tp)
         near = pltpu.make_async_copy(src, dst, here_sem)
-
-        @pl.when(dest != s)
+        stays = (section == s) & (tp == t)
+
+        @pl.when(jnp.logical_not(stays))
         def _():
             away.start()
 
-        @pl.when(dest == s)
+        @pl.when(stays)
         def _():
             near.start()
 
         def finish():
-            @pl.when(dest != s)
+            @pl.when(jnp.logical_not(stays))
             def _():
                 away.wait_send()
 
-            @pl.when(dest == s)
+            @pl.when(stays)
             def _():
                 near.wait()
 
-        return finish
-
-    ends = []
-
-    def joined_halves(p):
-        swap(p).wait_recv()
-        return partial[hi * 8 + z, p].astype(F32) + hland[p].astype(F32)
+        ends.append(finish)
 
     for p in range(PARTS):
         advance(p, STEPS)
-        go(swap(p))
-    for n in (2, 3, 4, 5):
-        x_copy(n).wait_recv()
-    for b in range(2):
-        wsum_ref[b] = acc[b, skip, :] + (dwl[2 + b].astype(F32) + dwl[4 + b].astype(F32))
-    for p in range(4):
-        total[p] = joined_halves(p).astype(BF16)
-        dest = (y * 4 + p + NSEC - 1) % NSEC
-        ends.append(move(total.at[p], pland.at[j], ps_sem.at[p], pr_sem.at[j], fin_sem.at[p], dest))
-    value = joined_halves(4)
-    for n in range(4):
-        etotal[n] = value[:, n * HD : (n + 1) * HD]
-        dest = 2 * j + n % 2 + 8 * (n // 2)
-        ends.append(
-            move(etotal.at[n], eland.at[y], es_sem.at[n], er_sem.at[y], fin_sem.at[4 + n], dest)
+        if p == 1:
+            e_advance(STEPS - 1)
+        for d in range(2):
+            move(
+                partial.at[8 * d + z, p], pland.at[hi, j], ps_sem.at[d, p], pr_sem.at[hi, j],
+                fin_sem.at[d, p], (y * 4 + p + NSEC - 1) % NSEC, 8 * d + z,
+            )
+    e_advance(STEPS)
+    e_dest = 2 * j + y % 2 + 8 * (y // 2)
+    for d in range(2):
+        move(
+            epart.at[8 * d + z], efin.at[hi], es_sem.at[d], er_sem.at[hi],
+            fin_sem.at[d, PARTS], e_dest, 8 * d + z,
         )
     n_copy.wait_recv()
-    for n in range(4):
-        source = (((s + 1) % NSEC) // 4) * 4 + n
-
-        @pl.when(source != s)
-        def _():
-            remote(total.at[n], pland.at[n], ps_sem.at[n], pr_sem.at[n], source, t).wait_recv()
+    for h in range(2):
+        for n in range(4):
+            source = (((s + 1) % NSEC) // 4) * 4 + n
+
+            @pl.when((source != s) | (h != hi))
+            def _():
+                remote(
+                    partial.at[8 * h + z, n], pland.at[h, n], ps_sem.at[h, n], pr_sem.at[h, n],
+                    source, 8 * h + z,
+                ).wait_recv()
 
     for end in ends:
         end()
     more = jnp.where(s == NSEC - 1, 0.0, 1.0).astype(F32)
     for n in range(8):
-        half = pland[n % 4].astype(F32)[:, (n // 4) * COLS : (n // 4 + 1) * COLS]
+        cols = slice((n // 4) * COLS, (n // 4 + 1) * COLS)
+        half = (pland[0, n % 4].astype(F32) + pland[1, n % 4].astype(F32))[:, cols]
         passed_ref[:, n * COLS : (n + 1) * COLS] = (
             (nland[:, n * COLS : (n + 1) * COLS].astype(F32) + half) * more
         ).astype(BF16)
-    for n in range(4):
-        source = n * 4 + (s % 8) // 2
-
-        @pl.when(source != s)
+
+    for n in (2, 3, 4, 5):
+        x_copy(n).wait_recv()
+    for b in range(2):
+        came = dwl[2 + b].astype(F32) + dwl[4 + b].astype(F32)
+        for i in range(3):
+            cols = slice(i * RANK, (i + 1) * RANK)
+            wsum_ref[b, :, cols] = acc[b, skip, cols] + came[i * COLS : (i + 1) * COLS, :]
+        last = came[3 * COLS :, :]
+        wsum_ref[b, 0:HD, 3 * RANK : COLS] = acc[b, upper, 3 * RANK : COLS] + last[:, 0:64]
+        wsum_ref[b, HD:COLS, 3 * RANK : COLS] = acc[b, lower, 3 * RANK : COLS] + last[:, 64:RANK]
+    for h in range(2):
+        @pl.when((e_dest != s) | (h != hi))
         def _():
-            remote(etotal.at[n], eland.at[n], es_sem.at[n], er_sem.at[n], source, t).wait_recv()
-
-    embed_ref[...] = jnp.sum(eland[...], axis=0)
+            remote(
+                epart.at[8 * h + z], efin.at[h], es_sem.at[h], er_sem.at[h], e_dest, 8 * h + z
+            ).wait_recv()
+
+    embed_ref[...] = efin[0].astype(F32) + efin[1].astype(F32)
     for copy in sent:
         copy.wait_send()
 
@@ -528,23 +588,25 @@
             pltpu.VMEM((4, COLS, TOKENS), BF16),
             pltpu.VMEM((NTP, PARTS, 32, 2 * COLS), BF16),
             pltpu.VMEM((2, PARTS, STEPS, 32, 2 * COLS), BF16),
-            pltpu.VMEM((PARTS, 32, 2 * COLS), BF16),
-            pltpu.VMEM((4, 32, 2 * COLS), BF16),
-            pltpu.VMEM((4, 32, HD), F32),
-            pltpu.VMEM((4, 32, 2 * COLS), BF16),
-            pltpu.VMEM((4, 32, HD), F32),
+            pltpu.VMEM((2, 4, 32, 2 * COLS), BF16),
             pltpu.VMEM((32, WIDTH), BF16),
+            pltpu.VMEM((4, TOKENS, HD), BF16),
+            pltpu.VMEM((4, TOKENS, HD), BF16),
+            pltpu.VMEM((NTP, 32, HD), BF16),
+            pltpu.VMEM((2, STEPS, 32, HD), BF16),
+            pltpu.VMEM((2, 32, HD), BF16),
             pltpu.VMEM((TOKENS, 2 * COLS), F32),
             pltpu.VMEM((2, TOKENS, COLS), BF16),
             pltpu.VMEM((2, WIN, COLS), F32),
-            pltpu.VMEM((6, COLS, COLS), BF16),
-            pltpu.VMEM((6, COLS, COLS), BF16),
+            pltpu.VMEM((6, 3 * COLS + HD, RANK), BF16),
+            pltpu.VMEM((6, 3 * COLS + HD, RANK), BF16),
             dma((13,)), dma((6,)), dma((6,)), dma((10,)), dma((10,)), dma((3,)), dma((4,)),
             dma((15,)), dma((16,)), dma((15,)), dma((16,)),
             dma((2,)), dma((8,)),
             dma((2, PARTS, STEPS)), dma((2, PARTS, STEPS)),
-            dma((PARTS,)), dma((PARTS,)), dma((6,)), dma((6,)),
-            dma((4,)), dma((4,)), dma((4,)), dma((4,)), dma((8,)), dma((2,)),
+            dma((6,)), dma((6,)),
+            dma((2, 4)), dma((2, 4)), dma((2,)), dma((2,)), dma((2, PARTS + 1)), dma((2,)),
+            dma((3,)), dma((4,)), dma((2, STEPS)), dma((2, STEPS)),
         ],
         compiler_params=pltpu.CompilerParams(
             collective_id=0, has_side_effects=True, vmem_limit_bytes=VMEM_LIMIT
@@ -557,13 +619,28 @@
     count = (len(refs) - 1) // 3
     sems = refs[-1]
     ins, outs, held = refs[:count], refs[count : 2 * count], refs[2 * count : 3 * count]
-    coming = [pltpu.make_async_copy(ins[n], held[n], sems.at[0, n]) for n in range(count)]
-    going = [pltpu.make_async_copy(held[n], outs[n], sems.at[1, n]) for n in range(count)]
+    pieces = []
+    for n in range(count):
+        rows = ins[n].shape[-2]
+        if len(ins[n].shape) == 3:
+            pieces += [(n, (b, pl.ds(h * HD, HD))) for b in range(2) for h in range(2)]
+        elif rows == COLS:
+            pieces += [(n, (pl.ds(h * HD, HD),)) for h in range(2)]
+        else:
+            pieces.append((n, (pl.ds(0, rows),)))
+
+    def copies(a, b, side):
+        return [
+            pltpu.make_async_copy(a[n].at[at], b[n].at[at], sems.at[side, m])
+            for m, (n, at) in enumerate(pieces)
+        ]
+
+    coming, going = copies(ins, held, 0), copies(held, outs, 1)
     for copy in coming:
         copy.start()
-    for n in range(count):
-        coming[n].wait()
-        going[n].start()
+    for here, on in zip(coming, going):
+        here.wait()
+        on.start()
     for copy in going:
         copy.wait()
 
@@ -576,7 +653,7 @@
         in_specs=[anys] * len(arrays),
         out_specs=(anys,) * len(arrays),
         scratch_shapes=[pltpu.VMEM(a.shape, a.dtype) for a in arrays]
-        + [pltpu.SemaphoreType.DMA((2, len(arrays)))],
+        + [pltpu.SemaphoreType.DMA((2, 16))],
         compiler_params=pltpu.CompilerParams(vmem_limit_bytes=VMEM_LIMIT),
         name="hand_over",
     )(*arrays)

time: 109 us -> 106 us (0.972)
  Pallas kernels: 109 us -> 105 us
    pallas_call x1, Pallas kernels: 105 us -> 102 us  [whole_call(): pl.pallas_call(whole_kernel, out_shape=(out((COLS, TOKENS), BF16), out((C...]
where the time goes in v5:
time: 106 us
  Pallas kernels  105 us (99%)
    pallas_call x1, Pallas kernels, whole_call(): pl.pallas_call(whole_kernel, out_shape=(out((COLS, TOKENS), BF16), out((C...  102 us
    pallas_call x1, Pallas kernels, copy_call(): pl.pallas_call(copy_kernel, out_shape=tuple((jax.ShapeDtypeStruct(a.shape...  3.51 us

profile of v5, /device:TPU:1, one launch (start us, length us, event | category | flops | bytes accessed | tf_op | source)
XLA Modules:
  0.0 106.1 jit_solution(15460377764284010428)
XLA Ops:
  0.6 101.8 %attention_block_backward.1 = (bf16[448,512]{1,0:T(8,128)(2,1)}, bf16[448,512]{1,0:T(8,128)(2,1)}, f32[448,128]{1,0:T(8,128)}, f32[448,128]{1,0:T(8,128)}, f32[2...) custom-call(s32[16]{0:T(128)} %bitcast.40, bf16[448,512]{1,0:T(8,128)(2,1)} %bitcast.32, ...), custom_call_target="tpu_custom_call" | custom-call | tf_op jit(solution)/shard_map/attention_block_backward/pallas_call | solution.py:560
  102.4 3.5 %hand_over.1 = (bf16[448,512]{1,0:T(8,128)(2,1)}, bf16[448,512]{1,0:T(8,128)(2,1)}, f32[448,128]{1,0:T(8,128)}, f32[448,128]{1,0:T(8,128)}, f32[2,448,448]{2,1,0...) custom-call(bf16[448,512]{1,0:T(8,128)(2,1)} %get-tuple-element.21.refs_0_, ...), custom_call_target="tpu_custom_call" | custom-call | tf_op jit(solution)/shard_map/hand_over/pallas_call | solution.py:650
